TPU v7x, 32 devices: a whole 2x2x4 slice. The times are simulated.
32 devices in a mesh: seq: 8 (over y, x, core), db: 4 (over z).
Axes of the slice: x: 2, y: 2, z: 4, core: 2. Of those that a mesh axis runs over, the one named last changes fastest.
Arguments:
- decoder: bfloat16 [8192, 4096], P('seq'), may hold values from -6 to 6
- w_query: bfloat16 [4096, 4096], P(None, 'db'), may hold values from -0.09375 to 0.09375
- w_key: bfloat16 [896, 4096], P(None, 'db'), may hold values from -0.1875 to 0.1875
- w_value: bfloat16 [896, 4096], P(None, 'db'), may hold values from -0.1875 to 0.1875
- w_out: bfloat16 [4096, 4096], P('db'), may hold values from -0.09375 to 0.09375
- database: bfloat16 [192, 128, 896], P('seq'), may hold values from -240 to 240
- nb_shard: int32 [128, 2], replicated, may hold values from 0 to 7, as said below
- nb_slot: int32 [128, 2], replicated, may hold values from 0 to 23
Outputs:
- attended: bfloat16 [8192, 4096], P(('seq', 'db'))
Inputs may be any that keep to these rules, and one draw needn't show every extreme that they name: `nb_shard`: the 32 entries of each 16 consecutive spans name any one shard at most 5 times, and one shard exactly 5 times.
All inputs are finite; a program needn't handle non-finite values.
Results may differ from a plain program's by a relative error of at most 0.022.
The roundings to bfloat16 on the way count: a program that leaves them out, or rounds other values in their place, can miss the bound.
Values may be sent and summed in bfloat16 or wider, within the bound.
A program may use at most 128 MiB of HBM per device.

v0:
```python
import math

import jax
import jax.numpy as jnp
from jax import lax
from jax.sharding import PartitionSpec as P

HS = 128
CL = 64
NB_LEN = 128
NEIGH = 2


def shifted(value, axis, steps):
    count = lax.axis_size(axis)
    first, last = (max(0, -steps), min(count, count - steps))
    return lax.ppermute(value, axis, [(source, source + steps) for source in range(first, last)])


def attend(queries, keys, values):
    blocks, qlen, width = queries.shape
    heads_here = width // HS
    q_heads = queries.reshape(blocks, qlen, heads_here, HS)
    k_heads = keys.reshape(blocks, keys.shape[1], heads_here, HS)
    v_heads = values.reshape(blocks, values.shape[1], heads_here, HS)
    scores = jnp.einsum("bqhd,bkhd->bhqk", q_heads, k_heads, preferred_element_type=jnp.float32) * (
        1.0 / math.sqrt(HS)
    )
    probs = jax.nn.softmax(scores, axis=-1).astype(jnp.bfloat16)
    context = jnp.einsum("bhqk,bkhd->bqhd", probs, v_heads, preferred_element_type=jnp.float32)
    return context.reshape(blocks, qlen, width).astype(jnp.bfloat16)


def bucket_places(shards):
    count = shards.shape[1]
    same_shard = shards[:, :, None] == shards[:, None, :]
    earlier = jnp.arange(count)[None, :] < jnp.arange(count)[:, None]
    return jnp.sum((same_shard & earlier[None]).astype(jnp.int32), axis=2)


def body(decoder, w_query, w_key, w_value, w_out, database, nb_shard, nb_slot):
    n_seq = lax.axis_size("seq")
    seq_index = lax.axis_index("seq")
    tok_rows = decoder.shape[0]
    spans_dev = tok_rows // CL
    width = w_query.shape[1]
    requests = NEIGH * spans_dev
    capacity = (requests + n_seq - 1) // n_seq + 1
    source = decoder.astype(jnp.float32)
    scale = lax.rsqrt(jnp.mean(source * source, axis=-1, keepdims=True) + 1e-05)
    normed = (source * scale).astype(jnp.bfloat16)
    queries = jnp.dot(normed, w_query, preferred_element_type=jnp.float32).astype(jnp.bfloat16)
    shard_lists = nb_shard.reshape(n_seq, requests)
    slot_lists = nb_slot.reshape(n_seq, requests)
    places = bucket_places(shard_lists)
    mine = shard_lists == seq_index
    picked = mine[:, None, :] & (places[:, None, :] == jnp.arange(capacity)[None, :, None])
    send_slot = jnp.sum(jnp.where(picked, slot_lists[:, None, :], 0), axis=2)
    outgoing = database[send_slot]
    received = lax.all_to_all(outgoing, "seq", split_axis=0, concat_axis=0, tiled=True)
    my_shards = lax.dynamic_index_in_dim(shard_lists, seq_index, 0, keepdims=False)
    my_places = lax.dynamic_index_in_dim(places, seq_index, 0, keepdims=False)
    row_index = my_shards * capacity + my_places
    flat_received = received.reshape(n_seq * capacity, NB_LEN, received.shape[3])
    neighbour_rows = flat_received[row_index].reshape(spans_dev, NEIGH * NB_LEN, received.shape[3])
    keys = jnp.einsum(
        "cne,eh->cnh", neighbour_rows, w_key, preferred_element_type=jnp.float32
    ).astype(jnp.bfloat16)
    values = jnp.einsum(
        "cne,eh->cnh", neighbour_rows, w_value, preferred_element_type=jnp.float32
    ).astype(jnp.bfloat16)
    incoming = shifted(queries[: CL - 1], "seq", -1)
    aligned_queries = jnp.concatenate([queries[CL - 1 :], incoming], axis=0).reshape(
        spans_dev, CL, width
    )
    aligned = attend(aligned_queries, keys, values).reshape(tok_rows, width)
    leading = shifted(aligned[tok_rows - CL + 1 :], "seq", 1)
    context = jnp.concatenate([leading, aligned[: tok_rows - CL + 1]], axis=0)
    return lax.psum_scatter(
        jnp.dot(context, w_out, preferred_element_type=jnp.float32).astype(jnp.bfloat16),
        "db",
        scatter_dimension=0,
        tiled=True,
    )


def solution(mesh):
    return jax.shard_map(
        body,
        mesh=mesh,
        in_specs=(
            P("seq", None),
            P(None, "db"),
            P(None, "db"),
            P(None, "db"),
            P("db", None),
            P("seq", None, None),
            P(),
            P(),
        ),
        out_specs=P(("seq", "db"), None),
        check_vma=False,
    )
```

profile of v0, /device:TPU:0, one launch (start us, length us, event | category | flops | bytes accessed | tf_op | source)
XLA Modules:
  0.0 376.7 jit_solution(9434181455435046452)
XLA Ops:
  6.5 0.9 copy.18
  7.9 0.8 copy.19
  9.1 9.3 %gather_fusion = bf16[40,128,896]{2,1,0:T(8,128)(2,1)} fusion(bf16[24,128,896]{2,1,0:T(8,128)(2,1)} %param.13, s32[1024]{0:T(1024)S(1)} %pad_clamp_fusion.1), kind=kCustom, calls=%fused_computation | custom fusion | bytes 18350240 | tf_op jit(solution)/shard_map/gather | solution.py:59
  18.4 5.1 %all-to-all-start = ((bf16[8,5,128,896]{3,2,1,0:T(8,128)(2,1)}), bf16[8,5,128,896]{3,2,1,0:T(8,128)(2,1)}, u32[]{:S(2)}, u32[]{:S(2)}) async-start(bf16[8,5,128,896]{3,2,1,0:T(8,128)(2,1)} %bitcast.44), calls=%async_computation | async-start | bytes 18350080 | tf_op jit(solution)/shard_map/all_to_all | solution.py:60
  23.6 5.2 %fusion.1 = f32[1024]{0:T(1024)S(1)} fusion(bf16[1024,4096]{1,0:T(8,128)(2,1)} %param.8), kind=kLoop, calls=%fused_computation.5 | loop fusion | flops 12581888 | bytes 8392704 | tf_op jit(solution)/shard_map/reduce_sum | solution.py:50
  29.4 11.3 %fusion.23 = bf16[1024,1024]{1,0:T(8,128)(2,1)S(1)} fusion(bf16[4096,1024]{1,0:T(8,128)(2,1)} %param.9, bf16[1024,4096]{1,0:T(8,128)(2,1)S(1)} %copy-done.3, f32[1024]{0:T(1024)S(1)} %add_rsqrt_fusion), kind=kOutput, calls=%fused_computation.31 | convolution fusion | flops 8603566080 | bytes 18878464 | tf_op jit(solution)/shard_map/dot_general | solution.py:52
  40.7 1.3 copy-done.5
  42.0 1.3 collective-permute-start
  43.3 2.1 slice.20
  45.9 1.9 copy.27
  47.8 78.8 %all-to-all-done = bf16[8,5,128,896]{3,2,1,0:T(8,128)(2,1)} async-done(((bf16[8,5,128,896]{3,2,1,0:T(8,128)(2,1)}), bf16[8,5,128,896]{3,2,1,0:T(8,128)(2,1)}, u32[]{:S(2)}, u32[]{:S(2)}) %all-to-all-start) | async-done | bytes 9175072 | tf_op jit(solution)/shard_map/all_to_all | solution.py:60
  126.6 8.0 %gather_fusion.1 = bf16[32,128,896]{2,1,0:T(8,128)(2,1)} fusion(bf16[40,128,896]{2,1,0:T(8,128)(2,1)} %bitcast.2, s32[1024]{0:T(1024)S(1)} %pad_clamp_fusion), kind=kCustom, calls=%fused_computation.1 | custom fusion | bytes 14680192 | tf_op jit(solution)/shard_map/gather | solution.py:65
  134.6 14.4 %convert_bitcast_fusion = bf16[16,32,8,8,128]{4,3,2,1,0:T(8,128)(2,1)} fusion(bf16[16,256,896]{2,1,0:T(8,128)(2,1)} %bitcast.49, bf16[896,1024]{1,0:T(8,128)(2,1)S(1)} %copy-done), kind=kOutput, calls=%fused_computation.16 | convolution fusion | flops 7520387072 | bytes 17563648 | tf_op jit(solution)/shard_map/cne,eh->cnh/dot_general | solution.py:66
  149.0 6.4 %fusion.8 = f32[16,8,64,256]{3,2,1,0:T(8,128)S(1)} fusion(bf16[16,32,8,8,128]{4,3,2,1,0:T(8,128)(2,1)} %convert_bitcast_fusion, bf16[16,64,8,128]{3,2,1,0:T(8,128)(2,1)S(1)} %bitcast.47), kind=kOutput, calls=%fused_computation.11 | convolution fusion | flops 536870912 | bytes 18874368 | tf_op jit(solution)/shard_map/bqhd,bkhd->bhqk/dot_general | solution.py:26
  155.4 3.2 copy-done.4
  158.6 3.0 fusion.39
  161.6 14.3 %convert_bitcast_fusion.1 = bf16[16,32,8,8,128]{4,3,2,1,0:T(8,128)(2,1)} fusion(bf16[16,256,896]{2,1,0:T(8,128)(2,1)} %bitcast.50, bf16[896,1024]{1,0:T(8,128)(2,1)S(1)} %copy-done.6), kind=kOutput, calls=%fused_computation.18 | convolution fusion | flops 7520387072 | bytes 17563648 | tf_op jit(solution)/shard_map/cne,eh->cnh/dot_general | solution.py:69
  175.9 21.4 %convert_bitcast_fusion.2 = bf16[16,64,8,128]{3,1,2,0:T(8,128)(2,1)} fusion(bf16[16,32,8,8,128]{4,3,2,1,0:T(8,128)(2,1)} %convert_bitcast_fusion.1, f32[16,8,64]{2,1,0:T(8,128)S(1)} %fusion.39, f32[16,8,64,256]{3,2,1,0:T(8,128)} %copy-done.4), kind=kOutput, calls=%fused_computation.30 | convolution fusion | flops 548413696 | bytes 18907136 | tf_op jit(solution)/shard_map/bhqk,bkhd->bqhd/dot_general | solution.py:30
  197.2 3.4 copy.24
  200.6 0.6 copy.42
  201.3 4.4 %collective-permute-start.1 = (bf16[63,1024]{1,0:T(8,128)(2,1)S(1)}, bf16[63,1024]{1,0:T(8,128)(2,1)S(1)}, u32[]{:S(2)}, u32[]{:S(2)}) collective-permute-start(bf16[63,1024]{1,0:T(8,128)(2,1)S(1)} %slice.22), channel_id=1, source_target_pairs={{0,4},{4,8},{8,12},{12,16},{16,20},{20,24},{24,28},{1,5},{5,9},{9,... | collective-permute-start | bytes 387080 | tf_op jit(solution)/shard_map/ppermute | solution.py:17
  205.9 0.8 collective-permute-done.1
  206.7 14.6 %convolution_convert_fusion = bf16[1024,4096]{1,0:T(8,128)(2,1)} fusion(bf16[1024,4096]{1,0:T(8,128)(2,1)} %param.12, bf16[961,1024]{1,0:T(8,128)(2,1)S(1)} %slice.23, bf16[63,1024]{1,0:T(8,128)(2,1)S(1)} %collective-permute-done.1), kind=kOutput, calls=%fused_computation.19 | convolution fusion | flops 8598323200 | bytes 18874368 | tf_op jit(solution)/shard_map/dot_general | solution.py:80
  221.3 148.5 %reduce-scatter.2.cloned.1.call-done = bf16[256,4096]{1,0:T(8,128)(2,1)} async-done(((bf16[1024,4096]{1,0:T(8,128)(2,1)}), bf16[256,4096]{1,0:T(8,128)(2,1)}) %reduce-scatter.2.cloned.1.call-update) | async-done | bytes 2097168 | tf_op jit(solution)/shard_map/reduce_scatter | solution.py:79
  (32 shorter events, 2.1 us)
Async XLA Ops:
  6.5 128.1 %copy-start = (bf16[896,1024]{1,0:T(8,128)(2,1)S(1)}, bf16[896,1024]{1,0:T(8,128)(2,1)}, u32[]{:S(2)}) copy-start(bf16[896,1024]{1,0:T(8,128)(2,1)} %param.10) | copy-start | bytes 5505028
  18.4 108.2 %all-to-all-start = ((bf16[8,5,128,896]{3,2,1,0:T(8,128)(2,1)}), bf16[8,5,128,896]{3,2,1,0:T(8,128)(2,1)}, u32[]{:S(2)}, u32[]{:S(2)}) async-start(bf16[8,5,128,896]{3,2,1,0:T(8,128)(2,1)} %bitcast.44), calls=%async_computation | async-start | bytes 18350080 | tf_op jit(solution)/shard_map/all_to_all | solution.py:60
  23.5 346.3 %reduce-scatter.2.cloned.1.call-start = ((), (), s32[]{:S(2)}) async-start(), calls=%async_computation.2 | async-start | bytes 10485760 | tf_op jit(solution)/shard_map/reduce_scatter | solution.py:79
  23.6 5.8 %copy-start.3 = (bf16[1024,4096]{1,0:T(8,128)(2,1)S(1)}, bf16[1024,4096]{1,0:T(8,128)(2,1)}, u32[]{:S(2)}) copy-start(bf16[1024,4096]{1,0:T(8,128)(2,1)} %param.8) | copy-start | bytes 25165828
  40.7 1.3 copy-start.5
  42.0 3.4 collective-permute-start
  134.6 14.4 %copy-start.2 = (bf16[128,8,8,128]{3,2,1,0:T(8,128)(2,1)S(1)}, bf16[128,8,8,128]{3,2,1,0:T(8,128)(2,1)}, u32[]{:S(2)}) copy-start(bf16[128,8,8,128]{3,2,1,0:T(8,128)(2,1)} %copy.27) | copy-start | bytes 6291460
  155.4 3.2 copy-start.4
  158.6 3.0 copy-start.6
  201.3 5.4 %collective-permute-start.1 = (bf16[63,1024]{1,0:T(8,128)(2,1)S(1)}, bf16[63,1024]{1,0:T(8,128)(2,1)S(1)}, u32[]{:S(2)}, u32[]{:S(2)}) collective-permute-start(bf16[63,1024]{1,0:T(8,128)(2,1)S(1)} %slice.22), channel_id=1, source_target_pairs={{0,4},{4,8},{8,12},{12,16},{16,20},{20,24},{24,28},{1,5},{5,9},{9,... | collective-permute-start | bytes 387080 | tf_op jit(solution)/shard_map/ppermute | solution.py:17
  206.7 163.1 %copy-start.1 = (bf16[896,1024]{1,0:T(8,128)(2,1)S(1)}, bf16[896,1024]{1,0:T(8,128)(2,1)}, u32[]{:S(2)}) copy-start(bf16[896,1024]{1,0:T(8,128)(2,1)} %param.10) | copy-start | bytes 5505028
Sparse Core Ops, SparseCore 0:
  221.4 148.3 reduce-scatter.1
where the time goes:
time: 377 us
  waiting for transfers between devices  228 us (60%)
  matrix products  82.4 us (22%)
  local copies, waits for them, and re-layouts  32.5 us (9%)
  between operations  13.6 us (4%)
  starting transfers between devices  10.9 us (3%)
  other arithmetic  9.16 us (2%)
    reduce_scatter x1, waiting for transfers between devices, body(): lax.psum_scatter(jnp.dot(context, w_out, preferred_element_type=jnp.float...  148 us
    all_to_all x1, waiting for transfers between devices, body(): lax.all_to_all(outgoing, 'seq', split_axis=0, concat_axis=0, tiled=True)  78.8 us
    dot_general x1, matrix products, attend(): jnp.einsum('bhqk,bkhd->bqhd', probs, v_heads, preferred_element_type=jnp....  21.4 us
    dot_general x1, matrix products, body(): jnp.dot(context, w_out, preferred_element_type=jnp.float32)  14.6 us
    dot_general x1, matrix products, body(): jnp.einsum('cne,eh->cnh', neighbour_rows, w_key, preferred_element_type=j...  14.4 us
    dot_general x1, matrix products, body(): jnp.einsum('cne,eh->cnh', neighbour_rows, w_value, preferred_element_type...  14.3 us
    dot_general x1, matrix products, body(): jnp.dot(normed, w_query, preferred_element_type=jnp.float32)  11.3 us
    unnamed x18, local copies, waits for them, and re-layouts  9.33 us
  transfers between devices with their start and end apart: 4, of which 3 were waited for; matrix products, arithmetic and copies ran while one was open for 6% of the time, Pallas kernels for 0%

commit v1 on v0

v1 whole, which is shorter than its diff:
```python
import functools
import math

import jax
import jax.numpy as jnp
from jax import lax
from jax.experimental import pallas as pl
from jax.experimental.pallas import tpu as pltpu
from jax.sharding import PartitionSpec as P

HS = 128
CL = 64
NB_LEN = 128
NEIGH = 2


def shifted(value, axis, steps):
    count = lax.axis_size(axis)
    first, last = (max(0, -steps), min(count, count - steps))
    return lax.ppermute(value, axis, [(source, source + steps) for source in range(first, last)])


def bucket_places(shards):
    count = shards.shape[1]
    same_shard = shards[:, :, None] == shards[:, None, :]
    earlier = jnp.arange(count)[None, :] < jnp.arange(count)[:, None]
    return jnp.sum((same_shard & earlier[None]).astype(jnp.int32), axis=2)


def attend_kernel(spans, first, second, q_ref, rows0, rows1, wk_ref, wv_ref, o_ref):
    rows = jnp.concatenate([rows0[0], rows1[0]], axis=0)
    keys = jnp.dot(rows, wk_ref[...], preferred_element_type=jnp.float32).astype(jnp.bfloat16)
    values = jnp.dot(rows, wv_ref[...], preferred_element_type=jnp.float32).astype(jnp.bfloat16)
    queries = q_ref[0]
    for head in range(queries.shape[1] // HS):
        cut = slice(head * HS, (head + 1) * HS)
        scores = lax.dot_general(
            queries[:, cut],
            keys[:, cut],
            (((1,), (1,)), ((), ())),
            preferred_element_type=jnp.float32,
        ) * (1.0 / math.sqrt(HS))
        weights = jnp.exp(scores - jnp.max(scores, axis=-1, keepdims=True))
        probs = (weights / jnp.sum(weights, axis=-1, keepdims=True)).astype(jnp.bfloat16)
        o_ref[0, :, cut] = jnp.dot(
            probs, values[:, cut], preferred_element_type=jnp.float32
        ).astype(jnp.bfloat16)


def attend(spans, entries, queries, rows, w_key, w_value):
    count = spans.shape[0]
    _, qlen, width = queries.shape
    _, nb_len, depth = rows.shape
    grid_spec = pltpu.PrefetchScalarGridSpec(
        num_scalar_prefetch=3,
        grid=(count,),
        in_specs=[
            pl.BlockSpec((1, qlen, width), lambda g, s, a, b: (s[g], 0, 0)),
            pl.BlockSpec((1, nb_len, depth), lambda g, s, a, b: (a[g], 0, 0)),
            pl.BlockSpec((1, nb_len, depth), lambda g, s, a, b: (b[g], 0, 0)),
            pl.BlockSpec((depth, width), lambda g, s, a, b: (0, 0)),
            pl.BlockSpec((depth, width), lambda g, s, a, b: (0, 0)),
        ],
        out_specs=pl.BlockSpec((1, qlen, width), lambda g, s, a, b: (g, 0, 0)),
    )
    keys_len = NEIGH * nb_len
    return pl.pallas_call(
        attend_kernel,
        grid_spec=grid_spec,
        out_shape=jax.ShapeDtypeStruct((count, qlen, width), jnp.bfloat16),
        compiler_params=pltpu.CompilerParams(vmem_limit_bytes=40 * 1024 * 1024),
        cost_estimate=pl.CostEstimate(
            flops=count * (4 * keys_len * depth * width + 4 * qlen * keys_len * width),
            bytes_accessed=count * 2 * (keys_len * depth + 2 * qlen * width) + 4 * depth * width,
            transcendentals=count * qlen * keys_len * width // HS,
        ),
        name="attend",
    )(spans, entries[spans, 0], entries[spans, 1], queries, rows, rows, w_key, w_value)


def body(decoder, w_query, w_key, w_value, w_out, database, nb_shard, nb_slot):
    n_seq = lax.axis_size("seq")
    n_db = lax.axis_size("db")
    seq_index = lax.axis_index("seq")
    db_index = lax.axis_index("db")
    tok_rows = decoder.shape[0]
    spans_dev = tok_rows // CL
    width = w_query.shape[1]
    requests = NEIGH * spans_dev
    capacity = (requests + n_seq - 1) // n_seq + 1
    shard_lists = nb_shard.reshape(n_seq, requests)
    slot_lists = nb_slot.reshape(n_seq, requests)
    places = bucket_places(shard_lists)
    mine = shard_lists == seq_index
    picked = mine[:, None, :] & (places[:, None, :] == jnp.arange(capacity)[None, :, None])
    send_slot = jnp.sum(jnp.where(picked, slot_lists[:, None, :], 0), axis=2)
    outgoing = database[send_slot]
    received = lax.all_to_all(outgoing, "seq", split_axis=0, concat_axis=0, tiled=True)
    my_shards = lax.dynamic_index_in_dim(shard_lists, seq_index, 0, keepdims=False)
    my_places = lax.dynamic_index_in_dim(places, seq_index, 0, keepdims=False)
    entries = (my_shards * capacity + my_places).reshape(spans_dev, NEIGH)
    rows = received.reshape(n_seq * capacity, NB_LEN, received.shape[3])
    swap = [(source, source ^ 1) for source in range(n_db)]
    part = w_out.shape[0] // n_seq
    w_part = lax.dynamic_slice_in_dim(w_out, seq_index * part, part, 0)
    w_other = lax.all_gather(lax.ppermute(w_part, "db", swap), "seq", axis=0, tiled=True)
    source = decoder.astype(jnp.float32)
    scale = lax.rsqrt(jnp.mean(source * source, axis=-1, keepdims=True) + 1e-05)
    normed = (source * scale).astype(jnp.bfloat16)
    queries = jnp.dot(normed, w_query, preferred_element_type=jnp.float32).astype(jnp.bfloat16)
    incoming = shifted(queries[: CL - 1], "seq", -1)
    aligned_queries = jnp.concatenate([queries[CL - 1 :], incoming], axis=0).reshape(
        spans_dev, CL, width
    )
    blocks = n_db // 2
    block_spans = spans_dev // n_db
    chunks = 2 if block_spans % 2 == 0 else 1
    chunk_spans = block_spans // chunks
    steps = 2 * jnp.arange(blocks)

    def spans_of(owner, chunk):
        block = lax.rem(owner + steps, n_db)
        inner = chunk * chunk_spans + jnp.arange(chunk_spans)
        return (block[:, None] * block_spans + inner[None, :]).reshape(-1).astype(jnp.int32)

    done = [None] * chunks
    for chunk in reversed(range(chunks)):
        theirs = attend(
            spans_of(db_index ^ 1, chunk), entries, aligned_queries, rows, w_key, w_value
        )
        from_pair = lax.ppermute(theirs, "db", swap)
        ours = attend(spans_of(db_index, chunk), entries, aligned_queries, rows, w_key, w_value)
        size = chunk_spans * CL
        total = jnp.dot(
            ours.reshape(-1, width), w_out, preferred_element_type=jnp.float32
        ) + jnp.dot(from_pair.reshape(-1, width), w_other, preferred_element_type=jnp.float32)
        partial = total.astype(jnp.bfloat16).reshape(blocks, size, -1)
        result = partial[0].astype(jnp.float32)
        for step in range(1, blocks):
            pairs = [(source, (source + 2 * step) % n_db) for source in range(n_db)]
            result = result + lax.ppermute(partial[step], "db", pairs).astype(jnp.float32)
        done[chunk] = result.astype(jnp.bfloat16)
    flat = n_seq * n_db
    halo = lax.ppermute(
        done[-1][-(CL - 1) :], ("seq", "db"), [(source, source + 1) for source in range(flat - 1)]
    )
    return jnp.concatenate([halo] + done[:-1] + [done[-1][: -(CL - 1)]], axis=0)


def solution(mesh):
    return jax.shard_map(
        body,
        mesh=mesh,
        in_specs=(
            P("seq", None),
            P(None, "db"),
            P(None, "db"),
            P(None, "db"),
            P("db", None),
            P("seq", None, None),
            P(),
            P(),
        ),
        out_specs=P(("seq", "db"), None),
        check_vma=False,
    )
```

time: 377 us -> 376 us (level)
  Pallas kernels: 0 us -> 64 us
  matrix products: 82.4 us -> 34.8 us
  waiting for transfers between devices: 228 us -> 210 us
  local copies, waits for them, and re-layouts: 32.5 us -> 24.6 us
  starting transfers between devices: 10.9 us -> 17.9 us
    reduce_scatter x1 -> x0, waiting for transfers between devices: 148 us -> none  [body(): lax.psum_scatter(jnp.dot(context, w_out, preferred_element_type=jnp.float...]
    ppermute x0 -> x6, waiting for transfers between devices: none -> 112 us  [the longest x2 88.8 us: body(): lax.ppermute(partial[step], 'db', pairs).astype(jnp.float32)]
    pallas_call x0 -> x4, Pallas kernels: none -> 64 us  [attend(): pl.pallas_call(attend_kernel, grid_spec=grid_spec, out_shape=jax.ShapeDty...]
    dot_general x5 -> x4, matrix products: 71.1 us -> 20.8 us  [the longest x2 10.6 us: body(): jnp.dot(from_pair.reshape(-1, width), w_other, preferred_element_type=jnp...]
    all_to_all x1, waiting for transfers between devices: 78.8 us -> 98 us  [body(): lax.all_to_all(outgoing, 'seq', split_axis=0, concat_axis=0, tiled=True)]
    ppermute x0 -> x6, starting transfers between devices: none -> 11.4 us  [the longest x2 3.24 us: body(): lax.ppermute(partial[step], 'db', pairs).astype(jnp.float32)]
    ppermute x2 -> x1, starting transfers between devices: 5.73 us -> 1.47 us  [shifted(): lax.ppermute(value, axis, [(source, source + steps) for source in range(f...]
    gather x1 -> x8, local copies, waits for them, and re-layouts: 7.96 us -> 5.08 us  [the longest x4 2.54 us: attend(): entries[spans, 0]]
  transfers between devices with their start and end apart: 4 -> 9, of which waited for: 3 -> 4; matrix products, arithmetic and copies ran while one was open for 6% -> 17% of each run, Pallas kernels for 0% -> 17%
where the time goes in v1:
time: 376 us; the launch traced here: 375 us
  waiting for transfers between devices  210 us (56%)
  Pallas kernels  64 us (17%)
  matrix products  34.8 us (9%)
  local copies, waits for them, and re-layouts  24.6 us (7%)
  starting transfers between devices  17.9 us (5%)
  between operations  13.7 us (4%)
  other arithmetic  9.78 us (3%)
    all_to_all x1, waiting for transfers between devices, body(): lax.all_to_all(outgoing, 'seq', split_axis=0, concat_axis=0, tiled=True)  98 us
    ppermute x2, waiting for transfers between devices, body(): lax.ppermute(partial[step], 'db', pairs).astype(jnp.float32)  88.8 us
    pallas_call x4, Pallas kernels, attend(): pl.pallas_call(attend_kernel, grid_spec=grid_spec, out_shape=jax.ShapeDty...  64 us
    ppermute x1, waiting for transfers between devices, body(): lax.ppermute(w_part, 'db', swap)  23.2 us
    dot_general x1, matrix products, body(): jnp.dot(normed, w_query, preferred_element_type=jnp.float32)  13.9 us
    dot_general x2, matrix products, body(): jnp.dot(from_pair.reshape(-1, width), w_other, preferred_element_type=jnp...  10.6 us
    dot_general x2, matrix products, body(): jnp.dot(ours.reshape(-1, width), w_out, preferred_element_type=jnp.float32)  10.3 us
    gather x1, local copies, waits for them, and re-layouts, body(): outgoing = database[send_slot]  9.43 us
  transfers between devices with their start and end apart: 9, of which 4 were waited for; matrix products, arithmetic and copies ran while one was open for 17% of the time, Pallas kernels for 17%

profile of v1, /device:TPU:0, one launch (start us, length us, event | category | flops | bytes accessed | tf_op | source)
XLA Modules:
  0.0 374.8 jit_solution(2357145905251807289)
XLA Ops:
  7.8 3.1 collective-permute-start.2
  10.9 23.2 %collective-permute-done.2 = bf16[128,4096]{1,0:T(8,128)(2,1)S(1)} collective-permute-done((bf16[128,4096]{1,0:T(8,128)(2,1)S(1)}, bf16[128,4096]{1,0:T(8,128)(2,1)S(1)}, u32[]{:S(2)}, u32[]{:S(2)}) %collective-permute-start.2) | collective-permute-done | bytes 1048608 | tf_op jit(solution)/shard_map/ppermute | solution.py:106
  37.5 9.4 %gather_fusion.2 = bf16[40,128,896]{2,1,0:T(8,128)(2,1)} fusion(bf16[24,128,896]{2,1,0:T(8,128)(2,1)} %param.13, s32[1024]{0:T(1024)S(1)} %pad_clamp_fusion), kind=kCustom, calls=%fused_computation.2 | custom fusion | bytes 18350240 | tf_op jit(solution)/shard_map/gather | solution.py:97
  47.0 5.0 %all-to-all-start = ((bf16[8,5,128,896]{3,2,1,0:T(8,128)(2,1)}), bf16[8,5,128,896]{3,2,1,0:T(8,128)(2,1)}, u32[]{:S(2)}, u32[]{:S(2)}) async-start(bf16[8,5,128,896]{3,2,1,0:T(8,128)(2,1)} %bitcast.42), calls=%async_computation | async-start | bytes 18350080 | tf_op jit(solution)/shard_map/all_to_all | solution.py:98
  52.0 5.1 %fusion = f32[1024]{0:T(1024)S(1)} fusion(bf16[1024,4096]{1,0:T(8,128)(2,1)} %param.8), kind=kLoop, calls=%fused_computation.11 | loop fusion | flops 12581888 | bytes 8392704 | tf_op jit(solution)/shard_map/reduce_sum | solution.py:108
  57.1 13.9 %fusion.7 = bf16[1024,1024]{1,0:T(8,128)(2,1)S(1)} fusion(bf16[4096,1024]{1,0:T(8,128)(2,1)} %param.9, bf16[1024,4096]{1,0:T(8,128)(2,1)} %param.8, f32[1024]{0:T(1024)S(1)} %add_rsqrt_fusion), kind=kOutput, calls=%fused_computation.23 | convolution fusion | flops 8603566080 | bytes 18878464 | tf_op jit(solution)/shard_map/dot_general | solution.py:110
  72.8 1.8 slice.54
  80.3 1.8 pad_maximum_fusion
  82.2 98.0 %all-to-all-done = bf16[8,5,128,896]{3,2,1,0:T(8,128)(2,1)} async-done(((bf16[8,5,128,896]{3,2,1,0:T(8,128)(2,1)}), bf16[8,5,128,896]{3,2,1,0:T(8,128)(2,1)}, u32[]{:S(2)}, u32[]{:S(2)}) %all-to-all-start) | async-done | bytes 9175072 | tf_op jit(solution)/shard_map/all_to_all | solution.py:98
  180.2 1.5 copy-done
  183.2 15.9 %attend.7 = bf16[4,64,1024]{2,1,0:T(8,128)(2,1)S(1)} custom-call(s32[4]{0:T(128)S(1)} %add.282.spans, s32[4]{0:T(128)S(1)} %gather_fusion.7, s32[4]{0:T(128)S(1)} %gather_fusion.8, bf16[16,64,1024]{2,1,0:T(8,128)(2,1)S(1)} %bitcast.36, bf16[40,128,896]{2,1,0:T(8,128)(2,1)} %bitcast.5.rows0.rows1, bf16[40,128,896]{2,1,0:T(8,128)(2,1)} %bitcast.5.rows0.rows1, ...), custom_call_target="tpu_custom_call" | custom-call | flops 4026531840 | bytes 6553600 | tf_op jit(solution)/shard_map/attend/pallas_call | solution.py:67
  199.1 1.6 collective-permute-start.5
  200.6 16.1 %attend.5 = bf16[4,64,1024]{2,1,0:T(8,128)(2,1)S(1)} custom-call(s32[4]{0:T(128)S(1)} %add.269.spans, s32[4]{0:T(128)S(1)} %gather_fusion.3, s32[4]{0:T(128)S(1)} %gather_fusion.4, bf16[16,64,1024]{2,1,0:T(8,128)(2,1)S(1)} %bitcast.37, bf16[40,128,896]{2,1,0:T(8,128)(2,1)} %bitcast.5.rows0.rows1, bf16[40,128,896]{2,1,0:T(8,128)(2,1)} %bitcast.5.rows0.rows1, ...), custom_call_target="tpu_custom_call" | custom-call | flops 4026531840 | bytes 6553600 | tf_op jit(solution)/shard_map/attend/pallas_call | solution.py:67
  217.4 16.0 %attend.4 = bf16[4,64,1024]{2,1,0:T(8,128)(2,1)S(1)} custom-call(s32[4]{0:T(128)S(1)} %add.255.spans, s32[4]{0:T(128)S(1)} %gather_fusion, s32[4]{0:T(128)S(1)} %gather_fusion.1, bf16[16,64,1024]{2,1,0:T(8,128)(2,1)S(1)} %bitcast.38, bf16[40,128,896]{2,1,0:T(8,128)(2,1)} %bitcast.5.rows0.rows1, bf16[40,128,896]{2,1,0:T(8,128)(2,1)} %bitcast.5.rows0.rows1, ...), custom_call_target="tpu_custom_call" | custom-call | flops 4026531840 | bytes 6553600 | tf_op jit(solution)/shard_map/attend/pallas_call | solution.py:67
  233.4 4.4 %fusion.30 = f32[256,4096]{1,0:T(8,128)} fusion(bf16[256,1024]{1,0:T(8,128)(2,1)S(1)} %bitcast.41, bf16[1024,4096]{1,0:T(8,128)(2,1)S(1)} %bitcast.44), kind=kOutput, calls=%fused_computation.73 | convolution fusion | flops 2147483648 | bytes 13107200 | tf_op jit(solution)/shard_map/dot_general | solution.py:134
  237.8 16.1 %attend.6 = bf16[4,64,1024]{2,1,0:T(8,128)(2,1)S(1)} custom-call(s32[4]{0:T(128)S(1)} %add.277.spans, s32[4]{0:T(128)S(1)} %gather_fusion.5, s32[4]{0:T(128)S(1)} %gather_fusion.6, bf16[16,64,1024]{2,1,0:T(8,128)(2,1)S(1)} %bitcast.39, bf16[40,128,896]{2,1,0:T(8,128)(2,1)} %bitcast.5.rows0.rows1, bf16[40,128,896]{2,1,0:T(8,128)(2,1)} %bitcast.5.rows0.rows1, ...), custom_call_target="tpu_custom_call" | custom-call | flops 4026531840 | bytes 6553600 | tf_op jit(solution)/shard_map/attend/pallas_call | solution.py:67
  253.9 7.1 %fusion.5 = bf16[256,4096]{1,0:T(8,128)(2,1)S(1)} fusion(f32[256,4096]{1,0:T(8,128)} %fusion.30, bf16[256,1024]{1,0:T(8,128)(2,1)} %bitcast.9, bf16[1024,4096]{1,0:T(8,128)(2,1)} %all-gather.2.cloned.1.call-done), kind=kOutput, calls=%fused_computation.17 | convolution fusion | flops 2149580800 | bytes 15204352 | tf_op jit(solution)/shard_map/dot_general | solution.py:136
  261.1 2.5 collective-permute-start.3
  263.5 5.9 %fusion.31 = f32[256,4096]{1,0:T(8,128)S(1)} fusion(bf16[256,1024]{1,0:T(8,128)(2,1)S(1)} %bitcast.40, bf16[1024,4096]{1,0:T(8,128)(2,1)} %param.12), kind=kOutput, calls=%fused_computation.74 | convolution fusion | flops 2147483648 | bytes 13107200 | tf_op jit(solution)/shard_map/dot_general | solution.py:134
  269.5 3.5 fusion.6
  273.8 58.5 %collective-permute-done.3 = bf16[128,4096]{1,0:T(8,128)(2,1)S(1)} collective-permute-done((bf16[128,4096]{1,0:T(8,128)(2,1)S(1)}, bf16[128,4096]{1,0:T(8,128)(2,1)S(1)}, u32[]{:S(2)}, u32[]{:S(2)}) %collective-permute-start.3) | collective-permute-done | bytes 1048608 | tf_op jit(solution)/shard_map/ppermute | solution.py:141
  332.7 3.0 collective-permute-start.4
  335.7 30.3 %collective-permute-done.6 = bf16[128,4096]{1,0:T(8,128)(2,1)S(1)} collective-permute-done((bf16[128,4096]{1,0:T(8,128)(2,1)S(1)}, bf16[128,4096]{1,0:T(8,128)(2,1)S(1)}, u32[]{:S(2)}, u32[]{:S(2)}) %collective-permute-start.6) | collective-permute-done | bytes 1048608 | tf_op jit(solution)/shard_map/ppermute | solution.py:141
  366.2 1.7 pad_maximum_fusion.1
  (73 shorter events, 15.9 us)
Async XLA Ops:
  6.5 247.3 %all-gather.2.cloned.1.call-start = ((), (), s32[]{:S(2)}) async-start(), calls=%async_computation.1 | async-start | bytes 9437184 | tf_op jit(solution)/shard_map/all_gather | solution.py:106
  7.8 26.2 %collective-permute-start.2 = (bf16[128,4096]{1,0:T(8,128)(2,1)S(1)}, bf16[128,4096]{1,0:T(8,128)(2,1)S(1)}, u32[]{:S(2)}, u32[]{:S(2)}) collective-permute-start(bf16[128,4096]{1,0:T(8,128)(2,1)S(1)} %constant_dynamic-slice_fusion), channel_id=1, source_target_pairs={{0,1},{1,0},{2,3},{3,2},{4,5},{5,4},{6,7},{7,6},{8,9},{9,8},{10,11... | collective-permute-start | bytes 3145736 | tf_op jit(solution)/shard_map/ppermute | solution.py:106
  34.1 1.0 copy-start.3
  47.0 133.2 %all-to-all-start = ((bf16[8,5,128,896]{3,2,1,0:T(8,128)(2,1)}), bf16[8,5,128,896]{3,2,1,0:T(8,128)(2,1)}, u32[]{:S(2)}, u32[]{:S(2)}) async-start(bf16[8,5,128,896]{3,2,1,0:T(8,128)(2,1)} %bitcast.42), calls=%async_computation | async-start | bytes 18350080 | tf_op jit(solution)/shard_map/all_to_all | solution.py:98
  71.1 9.3 %collective-permute-start = (bf16[63,1024]{1,0:T(8,128)(2,1)S(1)}, bf16[63,1024]{1,0:T(8,128)(2,1)S(1)}, u32[]{:S(2)}, u32[]{:S(2)}) collective-permute-start(bf16[63,1024]{1,0:T(8,128)(2,1)S(1)} %slice.55), channel_id=1, source_target_pairs={{4,0},{8,4},{12,8},{16,12},{20,16},{24,20},{28,24},{5,1},{9,5},{13... | collective-permute-start | bytes 387080 | tf_op jit(solution)/shard_map/ppermute | solution.py:20
  180.2 1.5 copy-start
  181.7 1.5 copy-start.2
  199.1 18.3 %copy-start.1 = (bf16[896,1024]{1,0:T(8,128)(2,1)S(1)}, bf16[896,1024]{1,0:T(8,128)(2,1)}, u32[]{:S(2)}) copy-start(bf16[896,1024]{1,0:T(8,128)(2,1)} %wk_ref.7) | copy-start | bytes 5505028
  199.1 70.3 %collective-permute-start.5 = (bf16[4,64,1024]{2,1,0:T(8,128)(2,1)S(1)}, bf16[4,64,1024]{2,1,0:T(8,128)(2,1)}, u32[]{:S(2)}, u32[]{:S(2)}) collective-permute-start(bf16[4,64,1024]{2,1,0:T(8,128)(2,1)S(1)} %attend.7), channel_id=1, source_target_pairs={{0,1},{1,0},{2,3},{3,2},{4,5},{5,4},{6,7},{7,6},{8,9},{9,8},{10,11... | collective-permute-start | bytes 1572872 | tf_op jit(solution)/shard_map/ppermute | solution.py:131
  200.6 32.7 %slice-start = ((s8[8388608]{0:T(1024)(128)(4,1)}), s8[4194304]{0:T(1024)(128)(4,1)S(1)}, s32[]{:S(2)}) async-start(s8[8388608]{0:T(1024)(128)(4,1)} %bitcast.43), calls=%async_computation.2 | async-start | bytes 8388608
  216.8 16.6 %slice-start.1 = ((s8[8388608]{0:T(1024)(128)(4,1)}), s8[4194304]{0:T(1024)(128)(4,1)S(1)}, s32[]{:S(2)}) async-start(s8[8388608]{0:T(1024)(128)(4,1)} %bitcast.43), calls=%async_computation.3 | async-start | bytes 8388608
  216.8 37.1 %collective-permute-start.1 = (bf16[4,64,1024]{2,1,0:T(8,128)(2,1)S(1)}, bf16[4,64,1024]{2,1,0:T(8,128)(2,1)}, u32[]{:S(2)}, u32[]{:S(2)}) collective-permute-start(bf16[4,64,1024]{2,1,0:T(8,128)(2,1)S(1)} %attend.5), channel_id=1, source_target_pairs={{0,1},{1,0},{2,3},{3,2},{4,5},{5,4},{6,7},{7,6},{8,9},{9,8},{10,11... | collective-permute-start | bytes 1572872 | tf_op jit(solution)/shard_map/ppermute | solution.py:131
  261.0 8.5 %slice-start.2 = ((s8[8388608]{0:T(1024)(128)(4,1)}), s8[4194304]{0:T(1024)(128)(4,1)S(1)}, s32[]{:S(2)}) async-start(s8[8388608]{0:T(1024)(128)(4,1)} %bitcast.45), calls=%async_computation.4 | async-start | bytes 8388608
  261.1 71.2 %collective-permute-start.3 = (bf16[128,4096]{1,0:T(8,128)(2,1)S(1)}, bf16[128,4096]{1,0:T(8,128)(2,1)S(1)}, u32[]{:S(2)}, u32[]{:S(2)}) collective-permute-start(bf16[128,4096]{1,0:T(8,128)(2,1)S(1)} %slice.57), channel_id=1, source_target_pairs={{0,2},{1,3},{2,0},{3,1},{4,6},{5,7},{6,4},{7,5},{8,10},{9,11},{10,... | collective-permute-start | bytes 3145736 | tf_op jit(solution)/shard_map/ppermute | solution.py:141
  263.5 5.9 %slice-start.3 = ((s8[8388608]{0:T(1024)(128)(4,1)}), s8[4194304]{0:T(1024)(128)(4,1)S(1)}, s32[]{:S(2)}) async-start(s8[8388608]{0:T(1024)(128)(4,1)} %bitcast.45), calls=%async_computation.5 | async-start | bytes 8388608
  273.0 92.9 %collective-permute-start.6 = (bf16[128,4096]{1,0:T(8,128)(2,1)S(1)}, bf16[128,4096]{1,0:T(8,128)(2,1)S(1)}, u32[]{:S(2)}, u32[]{:S(2)}) collective-permute-start(bf16[128,4096]{1,0:T(8,128)(2,1)S(1)} %slice.60), channel_id=1, source_target_pairs={{0,2},{1,3},{2,0},{3,1},{4,6},{5,7},{6,4},{7,5},{8,10},{9,11},{10,... | collective-permute-start | bytes 3145736 | tf_op jit(solution)/shard_map/ppermute | solution.py:141
  332.7 33.5 %collective-permute-start.4 = (bf16[63,4096]{1,0:T(8,128)(2,1)S(1)}, bf16[63,4096]{1,0:T(8,128)(2,1)S(1)}, u32[]{:S(2)}, u32[]{:S(2)}) collective-permute-start(bf16[63,4096]{1,0:T(8,128)(2,1)S(1)} %slice.58), channel_id=1, source_target_pairs={{0,1},{1,2},{2,3},{3,4},{4,5},{5,6},{6,7},{7,8},{8,9},{9,10},{10,1... | collective-permute-start | bytes 1548296 | tf_op jit(solution)/shard_map/ppermute | solution.py:144
Sparse Core Ops, SparseCore 0:
  35.2 120.3 all-gather.1

commit v2 on v1

v2 whole, which is shorter than its diff:
```python
import functools
import math

import jax
import jax.numpy as jnp
from jax import lax
from jax.experimental import pallas as pl
from jax.experimental.pallas import tpu as pltpu
from jax.sharding import PartitionSpec as P

HS = 128
CL = 64
NB_LEN = 128
NEIGH = 2


def shifted(value, axis, steps):
    count = lax.axis_size(axis)
    first, last = (max(0, -steps), min(count, count - steps))
    return lax.ppermute(value, axis, [(source, source + steps) for source in range(first, last)])


def bucket_places(shards):
    count = shards.shape[1]
    same_shard = shards[:, :, None] == shards[:, None, :]
    earlier = jnp.arange(count)[None, :] < jnp.arange(count)[:, None]
    return jnp.sum((same_shard & earlier[None]).astype(jnp.int32), axis=2)


def attend_kernel(spans, first, second, *refs):
    per_step = (len(refs) - 3) // 3
    q_refs, row_refs = refs[:per_step], refs[per_step : 3 * per_step]
    wk_ref, wv_ref, o_ref = refs[3 * per_step :]
    rows = jnp.concatenate([ref[0] for ref in row_refs], axis=0)
    keys = jnp.dot(rows, wk_ref[...], preferred_element_type=jnp.float32).astype(jnp.bfloat16)
    values = jnp.dot(rows, wv_ref[...], preferred_element_type=jnp.float32).astype(jnp.bfloat16)
    keys_len = keys.shape[0] // per_step
    for place in range(per_step):
        here = slice(place * keys_len, (place + 1) * keys_len)
        for head in range(keys.shape[1] // HS):
            cut = slice(head * HS, (head + 1) * HS)
            scores = lax.dot_general(
                q_refs[place][0, :, cut],
                keys[here, cut],
                (((1,), (1,)), ((), ())),
                preferred_element_type=jnp.float32,
            )
            top = jnp.max(scores, axis=-1, keepdims=True)
            weights = jnp.exp((scores - top) * (1.0 / math.sqrt(HS)))
            probs = weights * (1.0 / jnp.sum(weights, axis=-1, keepdims=True))
            o_ref[place, :, cut] = jnp.dot(
                probs.astype(jnp.bfloat16), values[here, cut], preferred_element_type=jnp.float32
            ).astype(jnp.bfloat16)


def attend(spans, entries, queries, rows, w_key, w_value):
    count = spans.shape[0]
    per_step = 2 if count % 2 == 0 else 1
    _, qlen, width = queries.shape
    _, nb_len, depth = rows.shape
    q_specs, row_specs = [], []
    for place in range(per_step):
        q_specs.append(
            pl.BlockSpec(
                (1, qlen, width), lambda g, s, a, b, place=place: (s[g * per_step + place], 0, 0)
            )
        )
        row_specs.append(
            pl.BlockSpec(
                (1, nb_len, depth), lambda g, s, a, b, place=place: (a[g * per_step + place], 0, 0)
            )
        )
        row_specs.append(
            pl.BlockSpec(
                (1, nb_len, depth), lambda g, s, a, b, place=place: (b[g * per_step + place], 0, 0)
            )
        )
    whole = pl.BlockSpec((depth, width), lambda g, s, a, b: (0, 0))
    grid_spec = pltpu.PrefetchScalarGridSpec(
        num_scalar_prefetch=3,
        grid=(count // per_step,),
        in_specs=q_specs + row_specs + [whole, whole],
        out_specs=pl.BlockSpec((per_step, qlen, width), lambda g, s, a, b: (g, 0, 0)),
    )
    keys_len = NEIGH * nb_len
    operands = [queries] * per_step + [rows] * (NEIGH * per_step) + [w_key, w_value]
    return pl.pallas_call(
        attend_kernel,
        grid_spec=grid_spec,
        out_shape=jax.ShapeDtypeStruct((count, qlen, width), jnp.bfloat16),
        compiler_params=pltpu.CompilerParams(vmem_limit_bytes=44 * 1024 * 1024),
        cost_estimate=pl.CostEstimate(
            flops=count * (4 * keys_len * depth * width + 4 * qlen * keys_len * width),
            bytes_accessed=count * 2 * (keys_len * depth + 2 * qlen * width) + 4 * depth * width,
            transcendentals=count * qlen * keys_len * width // HS,
        ),
        name="attend",
    )(spans, entries[spans, 0], entries[spans, 1], *operands)


def project_kernel(x_ref, y_ref, z_ref, wx_ref, wy_ref, wz_ref, rest_ref, last_ref):
    total = jnp.dot(x_ref[...], wx_ref[...], preferred_element_type=jnp.float32)
    total += jnp.dot(y_ref[...], wy_ref[...], preferred_element_type=jnp.float32)
    total += jnp.dot(z_ref[...], wz_ref[...], preferred_element_type=jnp.float32)
    total = total.astype(jnp.bfloat16)
    cut = rest_ref.shape[0]
    rest_ref[...] = total[:cut]
    last_ref[...] = total[cut:]


def project(x, y, z, w_x, w_y, w_z):
    size, width = x.shape
    features = w_x.shape[1]
    tile = 512
    own = lambda array: pl.BlockSpec(array.shape, lambda g: (0, 0))
    strip = lambda array: pl.BlockSpec((array.shape[0], tile), lambda g: (0, g))
    return pl.pallas_call(
        project_kernel,
        grid=(features // tile,),
        in_specs=[own(x), own(y), own(z), strip(w_x), strip(w_y), strip(w_z)],
        out_specs=[
            pl.BlockSpec((size - CL, tile), lambda g: (0, g)),
            pl.BlockSpec((CL, tile), lambda g: (0, g)),
        ],
        out_shape=[
            jax.ShapeDtypeStruct((size - CL, features), jnp.bfloat16),
            jax.ShapeDtypeStruct((CL, features), jnp.bfloat16),
        ],
        compiler_params=pltpu.CompilerParams(vmem_limit_bytes=40 * 1024 * 1024),
        cost_estimate=pl.CostEstimate(
            flops=4 * size * width * features,
            bytes_accessed=4 * width * features + 2 * size * features,
            transcendentals=0,
        ),
        name="project",
    )(x, y, z, w_x, w_y, w_z)


def body(decoder, w_query, w_key, w_value, w_out, database, nb_shard, nb_slot):
    n_seq = lax.axis_size("seq")
    n_db = lax.axis_size("db")
    seq_index = lax.axis_index("seq")
    db_index = lax.axis_index("db")
    tok_rows = decoder.shape[0]
    spans_dev = tok_rows // CL
    width = w_query.shape[1]
    requests = NEIGH * spans_dev
    capacity = (requests + n_seq - 1) // n_seq + 1
    shard_lists = nb_shard.reshape(n_seq, requests)
    slot_lists = nb_slot.reshape(n_seq, requests)
    places = bucket_places(shard_lists)
    mine = shard_lists == seq_index
    picked = mine[:, None, :] & (places[:, None, :] == jnp.arange(capacity)[None, :, None])
    send_slot = jnp.sum(jnp.where(picked, slot_lists[:, None, :], 0), axis=2)
    outgoing = database[send_slot]
    received = lax.all_to_all(outgoing, "seq", split_axis=0, concat_axis=0, tiled=True)
    my_shards = lax.dynamic_index_in_dim(shard_lists, seq_index, 0, keepdims=False)
    my_places = lax.dynamic_index_in_dim(places, seq_index, 0, keepdims=False)
    entries = (my_shards * capacity + my_places).reshape(spans_dev, NEIGH)
    rows = received.reshape(n_seq * capacity, NB_LEN, received.shape[3])
    swap = [(source, source ^ 1) for source in range(n_db)]
    half = w_out.shape[0] // 2
    my_half = lax.rem(seq_index, 2)
    w_near = lax.ppermute(
        lax.dynamic_slice_in_dim(w_out, my_half * half, half, 0), "db", swap
    )
    w_near, rows = lax.optimization_barrier((w_near, rows))
    w_far = lax.ppermute(w_near, "seq", [(source, source ^ 1) for source in range(n_seq)])
    source = decoder.astype(jnp.float32)
    scale = lax.rsqrt(jnp.mean(source * source, axis=-1, keepdims=True) + 1e-05)
    normed = (source * scale).astype(jnp.bfloat16)
    queries = jnp.dot(normed, w_query, preferred_element_type=jnp.float32).astype(jnp.bfloat16)
    incoming = shifted(queries[: CL - 1], "seq", -1)
    aligned_queries = jnp.concatenate([queries[CL - 1 :], incoming], axis=0).reshape(
        spans_dev, CL, width
    )
    blocks = n_db // 2
    block_spans = spans_dev // n_db

    def spans_of(owner, step):
        block = lax.rem(owner + 2 * step, n_db)
        return (block * block_spans + jnp.arange(block_spans)).astype(jnp.int32)

    def partial_of(step, queries):
        theirs = attend(spans_of(db_index ^ 1, step), entries, queries, rows, w_key, w_value)
        from_pair = lax.ppermute(theirs, "db", swap).reshape(-1, width)
        ours = attend(spans_of(db_index, step), entries, queries, rows, w_key, w_value)
        near = lax.dynamic_slice_in_dim(from_pair, my_half * half, half, 1)
        far = lax.dynamic_slice_in_dim(from_pair, (1 - my_half) * half, half, 1)
        return project(ours.reshape(-1, width), near, far, w_out, w_near, w_far)

    rests, lasts = [], []
    for step in range(1, blocks):
        rest, last = partial_of(step, aligned_queries)
        rest, last, aligned_queries = lax.optimization_barrier((rest, last, aligned_queries))
        pairs = [(source, (source + 2 * step) % n_db) for source in range(n_db)]
        lasts.append(lax.ppermute(last, "db", pairs))
        rests.append(lax.ppermute(rest, "db", pairs))
    rest, last = partial_of(0, aligned_queries)
    last = sum([value.astype(jnp.float32) for value in lasts], last.astype(jnp.float32))
    last = last.astype(jnp.bfloat16)
    flat = n_seq * n_db
    halo = lax.ppermute(
        last[1:], ("seq", "db"), [(source, source + 1) for source in range(flat - 1)]
    )
    rest = sum([value.astype(jnp.float32) for value in rests], rest.astype(jnp.float32))
    return jnp.concatenate([halo, rest.astype(jnp.bfloat16), last[:1]], axis=0)


def solution(mesh):
    return jax.shard_map(
        body,
        mesh=mesh,
        in_specs=(
            P("seq", None),
            P(None, "db"),
            P(None, "db"),
            P(None, "db"),
            P("db", None),
            P("seq", None, None),
            P(),
            P(),
        ),
        out_specs=P(("seq", "db"), None),
        check_vma=False,
    )
```

time: 376 us -> 333 us (0.89)
  waiting for transfers between devices: 210 us -> 169 us
  Pallas kernels: 64 us -> 86.2 us
  matrix products: 34.8 us -> 14 us
  between operations: 13.7 us -> 0.3 us
  local copies, waits for them, and re-layouts: 24.6 us -> 30.9 us
    all_to_all x1, waiting for transfers between devices: 98 us -> 6.38 us  [body(): lax.all_to_all(outgoing, 'seq', split_axis=0, concat_axis=0, tiled=True)]
    ppermute x6 -> x7, waiting for transfers between devices: 112 us -> 163 us  [the longest x1 91.2 us: body(): lax.ppermute(lax.dynamic_slice_in_dim(w_out, my_half * half, half, 0), 'd...]
    dot_general x4 -> x0, matrix products: 20.8 us -> none  [the longest x2 10.6 us: body(): jnp.dot(from_pair.reshape(-1, width), w_other, preferred_element_type=jnp...]
    pallas_call x0 -> x2, Pallas kernels: none -> 20.7 us  [project(): pl.pallas_call(project_kernel, grid=(features // tile,), in_specs=[own(x)...]
    unnamed x18 -> x20, local copies, waits for them, and re-layouts: 5.57 us -> 10.6 us
    ppermute x6 -> x7, starting transfers between devices: 11.4 us -> 12 us  [the longest x1 3.34 us: body(): lax.ppermute(last[1:], ('seq', 'db'), [(source, source + 1) for source in...]
  transfers between devices with their start and end apart: 9 -> 9, of which waited for: 4 -> 5; matrix products, arithmetic and copies ran while one was open for 17% -> 10% of each run, Pallas kernels for 17% -> 18%
where the time goes in v2:
time: 333 us; the launch traced here: 329 us
  waiting for transfers between devices  169 us (51%)
  Pallas kernels  86.2 us (26%)
  local copies, waits for them, and re-layouts  30.9 us (9%)
  starting transfers between devices  18.6 us (6%)
  matrix products  14 us (4%)
  other arithmetic  9.87 us (3%)
    ppermute x1, waiting for transfers between devices, body(): lax.ppermute(lax.dynamic_slice_in_dim(w_out, my_half * half, half, 0), 'd...  91.2 us
    pallas_call x4, Pallas kernels, attend(): pl.pallas_call(attend_kernel, grid_spec=grid_spec, out_shape=jax.ShapeDty...  65.5 us
    ppermute x1, waiting for transfers between devices, body(): lasts.append(lax.ppermute(last, 'db', pairs))  59.1 us
    pallas_call x2, Pallas kernels, project(): pl.pallas_call(project_kernel, grid=(features // tile,), in_specs=[own(x)...  20.7 us
    dot_general x1, matrix products, body(): jnp.dot(normed, w_query, preferred_element_type=jnp.float32)  14 us
    ppermute x1, waiting for transfers between devices, body(): lax.ppermute(last[1:], ('seq', 'db'), [(source, source + 1) for source in...  11.4 us
    unnamed x20, local copies, waits for them, and re-layouts  10.6 us
    gather x1, local copies, waits for them, and re-layouts, body(): outgoing = database[send_slot]  9.31 us
  transfers between devices with their start and end apart: 9, of which 5 were waited for; matrix products, arithmetic and copies ran while one was open for 10% of the time, Pallas kernels for 18%

profile of v2, /device:TPU:0, one launch (start us, length us, event | category | flops | bytes accessed | tf_op | source)
XLA Modules:
  0.0 328.8 jit_solution(13386062721014122261)
XLA Ops:
  2.4 9.3 %gather_fusion.4 = bf16[40,128,896]{2,1,0:T(8,128)(2,1)} fusion(bf16[24,128,896]{2,1,0:T(8,128)(2,1)} %param.13, s32[1024]{0:T(1024)S(1)} %pad_clamp_fusion), kind=kCustom, calls=%fused_computation.4 | custom fusion | bytes 18350240 | tf_op jit(solution)/shard_map/gather | solution.py:155
  11.8 5.2 %all-to-all-start = ((bf16[8,5,128,896]{3,2,1,0:T(8,128)(2,1)}), bf16[8,5,128,896]{3,2,1,0:T(8,128)(2,1)}, u32[]{:S(2)}, u32[]{:S(2)}) async-start(bf16[8,5,128,896]{3,2,1,0:T(8,128)(2,1)} %bitcast.38), calls=%async_computation | async-start | bytes 18350080 | tf_op jit(solution)/shard_map/all_to_all | solution.py:156
  16.9 2.5 constant_dynamic-slice_fusion.3
  19.4 3.0 collective-permute-start.1
  22.4 91.2 %collective-permute-done.1.wy_ref = bf16[512,4096]{1,0:T(8,128)(2,1)} collective-permute-done((bf16[512,4096]{1,0:T(8,128)(2,1)S(1)}, bf16[512,4096]{1,0:T(8,128)(2,1)}, u32[]{:S(2)}, u32[]{:S(2)}) %collective-permute-start.1) | collective-permute-done | bytes 4194336 | tf_op jit(solution)/shard_map/ppermute | solution.py:164
  113.6 6.4 %all-to-all-done = bf16[8,5,128,896]{3,2,1,0:T(8,128)(2,1)} async-done(((bf16[8,5,128,896]{3,2,1,0:T(8,128)(2,1)}), bf16[8,5,128,896]{3,2,1,0:T(8,128)(2,1)}, u32[]{:S(2)}, u32[]{:S(2)}) %all-to-all-start) | async-done | bytes 9175072 | tf_op jit(solution)/shard_map/all_to_all | solution.py:156
  119.9 5.1 %fusion = f32[1024]{0:T(1024)S(1)} fusion(bf16[1024,4096]{1,0:T(8,128)(2,1)} %param.8), kind=kLoop, calls=%fused_computation.11 | loop fusion | flops 12581888 | bytes 8392704 | tf_op jit(solution)/shard_map/reduce_sum | solution.py:170
  125.0 14.0 %fusion.5 = bf16[1024,1024]{1,0:T(8,128)(2,1)S(1)} fusion(bf16[4096,1024]{1,0:T(8,128)(2,1)} %param.9, bf16[1024,4096]{1,0:T(8,128)(2,1)} %param.8, f32[1024]{0:T(1024)S(1)} %add_rsqrt_fusion), kind=kOutput, calls=%fused_computation.18 | convolution fusion | flops 8603566080 | bytes 18878464 | tf_op jit(solution)/shard_map/dot_general | solution.py:172
  140.6 1.8 slice.34
  143.8 1.8 pad_maximum_fusion
  147.1 1.5 copy-done.4
  148.6 16.3 %attend.5 = bf16[4,64,1024]{2,1,0:T(8,128)(2,1)S(1)} custom-call(s32[4]{0:T(128)S(1)} %iota_add_fusion.1.spans, s32[4]{0:T(128)S(1)} %gather_fusion.5, s32[4]{0:T(128)S(1)} %gather_fusion.6, bf16[16,64,1024]{2,1,0:T(8,128)(2,1)S(1)} %bitcast.28, bf16[16,64,1024]{2,1,0:T(8,128)(2,1)S(1)} %bitcast.29, ...), custom_call_target="tpu_custom_call" | custom-call | flops 4026531840 | bytes 6553600 | tf_op jit(solution)/shard_map/attend/pallas_call | solution.py:87
  164.9 2.4 collective-permute-start.2
  169.9 1.5 copy-done.1
  172.9 16.3 %attend.4 = bf16[4,64,1024]{2,1,0:T(8,128)(2,1)S(1)} custom-call(s32[4]{0:T(128)S(1)} %iota_add_fusion.2.spans, s32[4]{0:T(128)S(1)} %gather_fusion.2, s32[4]{0:T(128)S(1)} %gather_fusion.3, bf16[16,64,1024]{2,1,0:T(8,128)(2,1)S(1)} %bitcast.30, bf16[16,64,1024]{2,1,0:T(8,128)(2,1)S(1)} %bitcast.31, ...), custom_call_target="tpu_custom_call" | custom-call | flops 4026531840 | bytes 6553600 | tf_op jit(solution)/shard_map/attend/pallas_call | solution.py:87
  189.3 10.4 %project.2 = (bf16[192,4096]{1,0:T(8,128)(2,1)S(1)}, bf16[64,4096]{1,0:T(8,128)(2,1)S(1)}) custom-call(bf16[256,1024]{1,0:T(8,128)(2,1)S(1)} %bitcast.37, bf16[256,512]{1,0:T(8,128)(2,1)S(1)} %get-tuple-element.26.y_ref, bf16[256,512]{1,0:T(8,128)(2,1)S(1)} %get-tuple-element.25.z_ref, bf16[1024,4096]{1,0:T(8,128)(2,1)} %wx_ref.3, ...), custom_call_target="tpu_custom_call" | custom-call | flops 4294967296 | bytes 18874368 | tf_op jit(solution)/shard_map/project/pallas_call | solution.py:117
  199.8 16.3 %attend.7 = bf16[4,64,1024]{2,1,0:T(8,128)(2,1)S(1)} custom-call(s32[4]{0:T(128)S(1)} %iota_add_fusion.spans, s32[4]{0:T(128)S(1)} %gather_fusion.7, s32[4]{0:T(128)S(1)} %gather_fusion.8, bf16[16,64,1024]{2,1,0:T(8,128)(2,1)S(1)} %bitcast.32, bf16[16,64,1024]{2,1,0:T(8,128)(2,1)S(1)} %bitcast.33, ...), custom_call_target="tpu_custom_call" | custom-call | flops 4026531840 | bytes 6553600 | tf_op jit(solution)/shard_map/attend/pallas_call | solution.py:87
  217.5 3.1 collective-permute-start.7
  223.7 16.5 %attend.6 = bf16[4,64,1024]{2,1,0:T(8,128)(2,1)S(1)} custom-call(s32[4]{0:T(128)S(1)} %iota_add_fusion.3.spans, s32[4]{0:T(128)S(1)} %gather_fusion, s32[4]{0:T(128)S(1)} %gather_fusion.1, bf16[16,64,1024]{2,1,0:T(8,128)(2,1)S(1)} %bitcast.34, bf16[16,64,1024]{2,1,0:T(8,128)(2,1)S(1)} %bitcast.35, ...), custom_call_target="tpu_custom_call" | custom-call | flops 4026531840 | bytes 6553600 | tf_op jit(solution)/shard_map/attend/pallas_call | solution.py:87
  242.1 10.2 %project.3 = (bf16[192,4096]{1,0:T(8,128)(2,1)S(1)}, bf16[64,4096]{1,0:T(8,128)(2,1)S(1)}) custom-call(bf16[256,1024]{1,0:T(8,128)(2,1)S(1)} %bitcast.36, bf16[256,512]{1,0:T(8,128)(2,1)S(1)} %get-tuple-element.24.y_ref, bf16[256,512]{1,0:T(8,128)(2,1)S(1)} %get-tuple-element.23.z_ref, bf16[1024,4096]{1,0:T(8,128)(2,1)} %wx_ref.3, ...), custom_call_target="tpu_custom_call" | custom-call | flops 4294967296 | bytes 18874368 | tf_op jit(solution)/shard_map/project/pallas_call | solution.py:117
  252.4 59.1 %collective-permute-done.5 = bf16[64,4096]{1,0:T(8,128)(2,1)S(1)} collective-permute-done((bf16[64,4096]{1,0:T(8,128)(2,1)S(1)}, bf16[64,4096]{1,0:T(8,128)(2,1)S(1)}, u32[]{:S(2)}, u32[]{:S(2)}) %collective-permute-start.5) | collective-permute-done | bytes 524320 | tf_op jit(solution)/shard_map/ppermute | solution.py:197
  311.8 3.3 %collective-permute-start.6 = (bf16[63,4096]{1,0:T(8,128)(2,1)S(1)}, bf16[63,4096]{1,0:T(8,128)(2,1)S(1)}, u32[]{:S(2)}, u32[]{:S(2)}) collective-permute-start(bf16[63,4096]{1,0:T(8,128)(2,1)S(1)} %slice.36), channel_id=1, source_target_pairs={{0,1},{1,2},{2,3},{3,4},{4,5},{5,6},{6,7},{7,8},{8,9},{9,10},{10,1... | collective-permute-start | bytes 1548296 | tf_op jit(solution)/shard_map/ppermute | solution.py:203
  315.7 11.4 %collective-permute-done.6 = bf16[63,4096]{1,0:T(8,128)(2,1)S(1)} collective-permute-done((bf16[63,4096]{1,0:T(8,128)(2,1)S(1)}, bf16[63,4096]{1,0:T(8,128)(2,1)S(1)}, u32[]{:S(2)}, u32[]{:S(2)}) %collective-permute-start.6) | collective-permute-done | bytes 516128 | tf_op jit(solution)/shard_map/ppermute | solution.py:203
  327.0 1.7 pad_maximum_fusion.1
  (63 shorter events, 18.1 us)
Async XLA Ops:
  11.8 108.2 %all-to-all-start = ((bf16[8,5,128,896]{3,2,1,0:T(8,128)(2,1)}), bf16[8,5,128,896]{3,2,1,0:T(8,128)(2,1)}, u32[]{:S(2)}, u32[]{:S(2)}) async-start(bf16[8,5,128,896]{3,2,1,0:T(8,128)(2,1)} %bitcast.38), calls=%async_computation | async-start | bytes 18350080 | tf_op jit(solution)/shard_map/all_to_all | solution.py:156
  19.4 94.2 %collective-permute-start.1 = (bf16[512,4096]{1,0:T(8,128)(2,1)S(1)}, bf16[512,4096]{1,0:T(8,128)(2,1)}, u32[]{:S(2)}, u32[]{:S(2)}) collective-permute-start(bf16[512,4096]{1,0:T(8,128)(2,1)S(1)} %constant_dynamic-slice_fusion.3), channel_id=1, source_target_pairs={{0,1},{1,0},{2,3},{3,2},{4,5},{5,4},{6,7},{7,6},{8,9},{9,8},{10,11... | collective-permute-start | bytes 12582920 | tf_op jit(solution)/shard_map/ppermute | solution.py:164
  119.9 69.3 %collective-permute-start.3 = (bf16[512,4096]{1,0:T(8,128)(2,1)}, bf16[512,4096]{1,0:T(8,128)(2,1)}, u32[]{:S(2)}, u32[]{:S(2)}) collective-permute-start(bf16[512,4096]{1,0:T(8,128)(2,1)} %collective-permute-done.1.wy_ref), channel_id=1, source_target_pairs={{0,4},{4,0},{8,12},{12,8},{16,20},{20,16},{24,28},{28,24},{1,5},{5... | collective-permute-start | bytes 12582920 | tf_op jit(solution)/shard_map/ppermute | solution.py:168
  139.0 4.7 %collective-permute-start = (bf16[63,1024]{1,0:T(8,128)(2,1)S(1)}, bf16[63,1024]{1,0:T(8,128)(2,1)S(1)}, u32[]{:S(2)}, u32[]{:S(2)}) collective-permute-start(bf16[63,1024]{1,0:T(8,128)(2,1)S(1)} %slice.35), channel_id=1, source_target_pairs={{4,0},{8,4},{12,8},{16,12},{20,16},{24,20},{28,24},{5,1},{9,5},{13... | collective-permute-start | bytes 387080 | tf_op jit(solution)/shard_map/ppermute | solution.py:20
  145.6 1.5 copy-start
  147.1 1.5 copy-start.4
  164.9 24.3 %collective-permute-start.2 = (bf16[4,64,1024]{2,1,0:T(8,128)(2,1)S(1)}, bf16[4,64,1024]{2,1,0:T(8,128)(2,1)S(1)}, u32[]{:S(2)}, u32[]{:S(2)}) collective-permute-start(bf16[4,64,1024]{2,1,0:T(8,128)(2,1)S(1)} %attend.5), channel_id=1, source_target_pairs={{0,1},{1,0},{2,3},{3,2},{4,5},{5,4},{6,7},{7,6},{8,9},{9,8},{10,11... | collective-permute-start | bytes 1572872 | tf_op jit(solution)/shard_map/ppermute | solution.py:186
  169.8 1.5 copy-start.1
  171.4 1.5 copy-start.5
  189.3 10.5 %copy-start.2 = (bf16[896,1024]{1,0:T(8,128)(2,1)S(1)}, bf16[896,1024]{1,0:T(8,128)(2,1)}, u32[]{:S(2)}) copy-start(bf16[896,1024]{1,0:T(8,128)(2,1)} %refs_6_.7) | copy-start | bytes 5505028
  189.3 10.5 %copy-start.6 = (bf16[896,1024]{1,0:T(8,128)(2,1)S(1)}, bf16[896,1024]{1,0:T(8,128)(2,1)}, u32[]{:S(2)}) copy-start(bf16[896,1024]{1,0:T(8,128)(2,1)} %refs_7_.7) | copy-start | bytes 5505028
  199.8 16.4 %copy-start.8 = (bf16[192,4096]{1,0:T(8,128)(2,1)}, bf16[192,4096]{1,0:T(8,128)(2,1)S(1)}, u32[]{:S(2)}) copy-start(bf16[192,4096]{1,0:T(8,128)(2,1)S(1)} %get-tuple-element.22) | copy-start | bytes 4718596
  216.1 24.9 %collective-permute-start.4 = (bf16[4,64,1024]{2,1,0:T(8,128)(2,1)S(1)}, bf16[4,64,1024]{2,1,0:T(8,128)(2,1)}, u32[]{:S(2)}, u32[]{:S(2)}) collective-permute-start(bf16[4,64,1024]{2,1,0:T(8,128)(2,1)S(1)} %attend.7), channel_id=1, source_target_pairs={{0,1},{1,0},{2,3},{3,2},{4,5},{5,4},{6,7},{7,6},{8,9},{9,8},{10,11... | collective-permute-start | bytes 1572872 | tf_op jit(solution)/shard_map/ppermute | solution.py:186
  217.5 97.6 %collective-permute-start.7 = (bf16[192,4096]{1,0:T(8,128)(2,1)}, bf16[192,4096]{1,0:T(8,128)(2,1)S(1)}, u32[]{:S(2)}, u32[]{:S(2)}) collective-permute-start(bf16[192,4096]{1,0:T(8,128)(2,1)} %copy-done.8), channel_id=1, source_target_pairs={{0,2},{1,3},{2,0},{3,1},{4,6},{5,7},{6,4},{7,5},{8,10},{9,11},{10,... | collective-permute-start | bytes 4718600 | tf_op jit(solution)/shard_map/ppermute | solution.py:198
  220.6 90.9 %collective-permute-start.5 = (bf16[64,4096]{1,0:T(8,128)(2,1)S(1)}, bf16[64,4096]{1,0:T(8,128)(2,1)S(1)}, u32[]{:S(2)}, u32[]{:S(2)}) collective-permute-start(bf16[64,4096]{1,0:T(8,128)(2,1)S(1)} %get-tuple-element.20), channel_id=1, source_target_pairs={{0,2},{1,3},{2,0},{3,1},{4,6},{5,7},{6,4},{7,5},{8,10},{9,11},{10,... | collective-permute-start | bytes 1572872 | tf_op jit(solution)/shard_map/ppermute | solution.py:197
  220.7 1.5 copy-start.3
  222.2 1.5 copy-start.7
  311.8 15.3 %collective-permute-start.6 = (bf16[63,4096]{1,0:T(8,128)(2,1)S(1)}, bf16[63,4096]{1,0:T(8,128)(2,1)S(1)}, u32[]{:S(2)}, u32[]{:S(2)}) collective-permute-start(bf16[63,4096]{1,0:T(8,128)(2,1)S(1)} %slice.36), channel_id=1, source_target_pairs={{0,1},{1,2},{2,3},{3,4},{4,5},{5,6},{6,7},{7,8},{8,9},{9,10},{10,1... | collective-permute-start | bytes 1548296 | tf_op jit(solution)/shard_map/ppermute | solution.py:203

commit v3 on v2

--- a/solution.py
+++ b/solution.py
@@ -27,75 +27,77 @@
     return jnp.sum((same_shard & earlier[None]).astype(jnp.int32), axis=2)
 
 
-def attend_kernel(spans, first, second, *refs):
+def attend_kernel(first, entries, *refs):
     per_step = (len(refs) - 3) // 3
     q_refs, row_refs = refs[:per_step], refs[per_step : 3 * per_step]
     wk_ref, wv_ref, o_ref = refs[3 * per_step :]
     rows = jnp.concatenate([ref[0] for ref in row_refs], axis=0)
     keys = jnp.dot(rows, wk_ref[...], preferred_element_type=jnp.float32).astype(jnp.bfloat16)
-    values = jnp.dot(rows, wv_ref[...], preferred_element_type=jnp.float32).astype(jnp.bfloat16)
-    keys_len = keys.shape[0] // per_step
-    for place in range(per_step):
-        here = slice(place * keys_len, (place + 1) * keys_len)
-        for head in range(keys.shape[1] // HS):
-            cut = slice(head * HS, (head + 1) * HS)
-            scores = lax.dot_general(
+    keys_len, qlen = keys.shape[0] // per_step, q_refs[0].shape[1]
+    units = [
+        (place, slice(place * keys_len, (place + 1) * keys_len), slice(at, at + HS))
+        for place in range(per_step)
+        for at in range(0, keys.shape[1], HS)
+    ]
+    scores = jnp.concatenate(
+        [
+            lax.dot_general(
                 q_refs[place][0, :, cut],
                 keys[here, cut],
                 (((1,), (1,)), ((), ())),
                 preferred_element_type=jnp.float32,
             )
-            top = jnp.max(scores, axis=-1, keepdims=True)
-            weights = jnp.exp((scores - top) * (1.0 / math.sqrt(HS)))
-            probs = weights * (1.0 / jnp.sum(weights, axis=-1, keepdims=True))
-            o_ref[place, :, cut] = jnp.dot(
-                probs.astype(jnp.bfloat16), values[here, cut], preferred_element_type=jnp.float32
-            ).astype(jnp.bfloat16)
-
-
-def attend(spans, entries, queries, rows, w_key, w_value):
-    count = spans.shape[0]
+            for place, here, cut in units
+        ],
+        axis=0,
+    )
+    values = jnp.dot(rows, wv_ref[...], preferred_element_type=jnp.float32).astype(jnp.bfloat16)
+    top = jnp.max(scores, axis=-1, keepdims=True)
+    weights = jnp.exp((scores - top) * (1.0 / math.sqrt(HS)))
+    probs = weights * (1.0 / jnp.sum(weights, axis=-1, keepdims=True))
+    probs = probs.astype(jnp.bfloat16)
+    for at, (place, here, cut) in enumerate(units):
+        o_ref[place, :, cut] = jnp.dot(
+            probs[at * qlen : (at + 1) * qlen],
+            values[here, cut],
+            preferred_element_type=jnp.float32,
+        ).astype(jnp.bfloat16)
+
+
+def attend(first, count, entries, queries, rows, w_key, w_value):
     per_step = 2 if count % 2 == 0 else 1
     _, qlen, width = queries.shape
     _, nb_len, depth = rows.shape
-    q_specs, row_specs = [], []
-    for place in range(per_step):
-        q_specs.append(
-            pl.BlockSpec(
-                (1, qlen, width), lambda g, s, a, b, place=place: (s[g * per_step + place], 0, 0)
-            )
+
+    def query_block(place):
+        return pl.BlockSpec(
+            (1, qlen, width), lambda g, f, e: (f[0] + g * per_step + place, 0, 0)
         )
-        row_specs.append(
-            pl.BlockSpec(
-                (1, nb_len, depth), lambda g, s, a, b, place=place: (a[g * per_step + place], 0, 0)
-            )
+
+    def row_block(place, which):
+        return pl.BlockSpec(
+            (1, nb_len, depth),
+            lambda g, f, e: (e[(f[0] + g * per_step + place) * NEIGH + which], 0, 0),
         )
-        row_specs.append(
-            pl.BlockSpec(
-                (1, nb_len, depth), lambda g, s, a, b, place=place: (b[g * per_step + place], 0, 0)
-            )
-        )
-    whole = pl.BlockSpec((depth, width), lambda g, s, a, b: (0, 0))
+
+    whole = pl.BlockSpec((depth, width), lambda g, f, e: (0, 0))
     grid_spec = pltpu.PrefetchScalarGridSpec(
-        num_scalar_prefetch=3,
+        num_scalar_prefetch=2,
         grid=(count // per_step,),
-        in_specs=q_specs + row_specs + [whole, whole],
-        out_specs=pl.BlockSpec((per_step, qlen, width), lambda g, s, a, b: (g, 0, 0)),
-    )
-    keys_len = NEIGH * nb_len
+        in_specs=[query_block(place) for place in range(per_step)]
+        + [row_block(place, which) for place in range(per_step) for which in range(NEIGH)]
+        + [whole, whole],
+        out_specs=pl.BlockSpec((per_step, qlen, width), lambda g, f, e: (g, 0, 0)),
+    )
     operands = [queries] * per_step + [rows] * (NEIGH * per_step) + [w_key, w_value]
     return pl.pallas_call(
         attend_kernel,
         grid_spec=grid_spec,
         out_shape=jax.ShapeDtypeStruct((count, qlen, width), jnp.bfloat16),
-        compiler_params=pltpu.CompilerParams(vmem_limit_bytes=44 * 1024 * 1024),
-        cost_estimate=pl.CostEstimate(
-            flops=count * (4 * keys_len * depth * width + 4 * qlen * keys_len * width),
-            bytes_accessed=count * 2 * (keys_len * depth + 2 * qlen * width) + 4 * depth * width,
-            transcendentals=count * qlen * keys_len * width // HS,
-        ),
+        compiler_params=pltpu.CompilerParams(vmem_limit_bytes=56 * 1024 * 1024),
+        cost_estimate=pl.CostEstimate(flops=1000, bytes_accessed=1000, transcendentals=0),
         name="attend",
-    )(spans, entries[spans, 0], entries[spans, 1], *operands)
+    )(first.reshape(1).astype(jnp.int32), entries, *operands)
 
 
 def project_kernel(x_ref, y_ref, z_ref, wx_ref, wy_ref, wz_ref, rest_ref, last_ref):
@@ -127,11 +129,7 @@
             jax.ShapeDtypeStruct((CL, features), jnp.bfloat16),
         ],
         compiler_params=pltpu.CompilerParams(vmem_limit_bytes=40 * 1024 * 1024),
-        cost_estimate=pl.CostEstimate(
-            flops=4 * size * width * features,
-            bytes_accessed=4 * width * features + 2 * size * features,
-            transcendentals=0,
-        ),
+        cost_estimate=pl.CostEstimate(flops=1000, bytes_accessed=1000, transcendentals=0),
         name="project",
     )(x, y, z, w_x, w_y, w_z)
 
@@ -156,7 +154,7 @@
     received = lax.all_to_all(outgoing, "seq", split_axis=0, concat_axis=0, tiled=True)
     my_shards = lax.dynamic_index_in_dim(shard_lists, seq_index, 0, keepdims=False)
     my_places = lax.dynamic_index_in_dim(places, seq_index, 0, keepdims=False)
-    entries = (my_shards * capacity + my_places).reshape(spans_dev, NEIGH)
+    entries = my_shards * capacity + my_places
     rows = received.reshape(n_seq * capacity, NB_LEN, received.shape[3])
     swap = [(source, source ^ 1) for source in range(n_db)]
     half = w_out.shape[0] // 2
@@ -164,8 +162,6 @@
     w_near = lax.ppermute(
         lax.dynamic_slice_in_dim(w_out, my_half * half, half, 0), "db", swap
     )
-    w_near, rows = lax.optimization_barrier((w_near, rows))
-    w_far = lax.ppermute(w_near, "seq", [(source, source ^ 1) for source in range(n_seq)])
     source = decoder.astype(jnp.float32)
     scale = lax.rsqrt(jnp.mean(source * source, axis=-1, keepdims=True) + 1e-05)
     normed = (source * scale).astype(jnp.bfloat16)
@@ -174,17 +170,20 @@
     aligned_queries = jnp.concatenate([queries[CL - 1 :], incoming], axis=0).reshape(
         spans_dev, CL, width
     )
+    w_near, rows, aligned_queries = lax.optimization_barrier((w_near, rows, aligned_queries))
+    near_seq = [(source, source ^ 1) for source in range(n_seq)]
+    w_far = lax.ppermute(w_near, "seq", near_seq)
     blocks = n_db // 2
     block_spans = spans_dev // n_db
 
-    def spans_of(owner, step):
-        block = lax.rem(owner + 2 * step, n_db)
-        return (block * block_spans + jnp.arange(block_spans)).astype(jnp.int32)
+    def attend_block(owner, step, queries):
+        first = lax.rem(owner + 2 * step, n_db) * block_spans
+        return attend(first, block_spans, entries, queries, rows, w_key, w_value)
 
     def partial_of(step, queries):
-        theirs = attend(spans_of(db_index ^ 1, step), entries, queries, rows, w_key, w_value)
+        theirs = attend_block(db_index ^ 1, step, queries)
         from_pair = lax.ppermute(theirs, "db", swap).reshape(-1, width)
-        ours = attend(spans_of(db_index, step), entries, queries, rows, w_key, w_value)
+        ours = attend_block(db_index, step, queries)
         near = lax.dynamic_slice_in_dim(from_pair, my_half * half, half, 1)
         far = lax.dynamic_slice_in_dim(from_pair, (1 - my_half) * half, half, 1)
         return project(ours.reshape(-1, width), near, far, w_out, w_near, w_far)
@@ -192,7 +191,6 @@
     rests, lasts = [], []
     for step in range(1, blocks):
         rest, last = partial_of(step, aligned_queries)
-        rest, last, aligned_queries = lax.optimization_barrier((rest, last, aligned_queries))
         pairs = [(source, (source + 2 * step) % n_db) for source in range(n_db)]
         lasts.append(lax.ppermute(last, "db", pairs))
         rests.append(lax.ppermute(rest, "db", pairs))

time: 333 us -> 282 us (0.85)
  Pallas kernels: 86.2 us -> 60.5 us
  local copies, waits for them, and re-layouts: 30.9 us -> 16.6 us
  waiting for transfers between devices: 169 us -> 162 us
    pallas_call x4, Pallas kernels: 65.5 us -> 40 us  [attend(): pl.pallas_call(attend_kernel, grid_spec=grid_spec, out_shape=jax.ShapeDty...]
    ppermute x1, waiting for transfers between devices: 91.2 us -> 73.3 us  [body(): lax.ppermute(lax.dynamic_slice_in_dim(w_out, my_half * half, half, 0), 'd...]
    ppermute x1, waiting for transfers between devices: 59.1 us -> 68 us  [body(): lasts.append(lax.ppermute(last, 'db', pairs))]
    unnamed x20 -> x8, local copies, waits for them, and re-layouts: 10.6 us -> 3.65 us
    gather x8 -> x0, local copies, waits for them, and re-layouts: 5.09 us -> none  [the longest x4 2.55 us: attend(): entries[spans, 0]]
    reduce_sum x1, other arithmetic: 5.07 us -> 1.69 us  [body(): scale = lax.rsqrt(jnp.mean(source * source, axis=-1, keepdims=True) + 1e-05)]
  transfers between devices with their start and end apart: 9 -> 9, of which waited for: 5 -> 6; matrix products, arithmetic and copies ran while one was open for 10% -> 7% of each run, Pallas kernels for 18% -> 18%
where the time goes in v3:
time: 282 us; the launch traced here: 278 us
  waiting for transfers between devices  162 us (57%)
  Pallas kernels  60.5 us (21%)
  starting transfers between devices  19.3 us (7%)
  local copies, waits for them, and re-layouts  16.6 us (6%)
  matrix products  11.3 us (4%)
  other arithmetic  8.1 us (3%)
    ppermute x1, waiting for transfers between devices, body(): lax.ppermute(lax.dynamic_slice_in_dim(w_out, my_half * half, half, 0), 'd...  73.3 us
    ppermute x1, waiting for transfers between devices, body(): lasts.append(lax.ppermute(last, 'db', pairs))  68 us
    pallas_call x4, Pallas kernels, attend(): pl.pallas_call(attend_kernel, grid_spec=grid_spec, out_shape=jax.ShapeDty...  40 us
    pallas_call x2, Pallas kernels, project(): pl.pallas_call(project_kernel, grid=(features // tile,), in_specs=[own(x)...  20.5 us
    dot_general x1, matrix products, body(): jnp.dot(normed, w_query, preferred_element_type=jnp.float32)  11.3 us
    ppermute x1, waiting for transfers between devices, body(): lax.ppermute(last[1:], ('seq', 'db'), [(source, source + 1) for source in...  9.36 us
    gather x1, local copies, waits for them, and re-layouts, body(): outgoing = database[send_slot]  9.25 us
    all_to_all x1, waiting for transfers between devices, body(): lax.all_to_all(outgoing, 'seq', split_axis=0, concat_axis=0, tiled=True)  6.26 us
  transfers between devices with their start and end apart: 9, of which 6 were waited for; matrix products, arithmetic and copies ran while one was open for 7% of the time, Pallas kernels for 18%

profile of v3, /device:TPU:0, one launch (start us, length us, event | category | flops | bytes accessed | tf_op | source)
XLA Modules:
  0.0 278.0 jit_solution(2332079183850419028)
XLA Ops:
  2.4 9.3 %gather_fusion = bf16[40,128,896]{2,1,0:T(8,128)(2,1)} fusion(bf16[24,128,896]{2,1,0:T(8,128)(2,1)} %param.13, s32[1024]{0:T(1024)S(1)} %pad_clamp_fusion), kind=kCustom, calls=%fused_computation | custom fusion | bytes 18350240 | tf_op jit(solution)/shard_map/gather | solution.py:153
  11.7 5.2 %all-to-all-start = ((bf16[8,5,128,896]{3,2,1,0:T(8,128)(2,1)}), bf16[8,5,128,896]{3,2,1,0:T(8,128)(2,1)}, u32[]{:S(2)}, u32[]{:S(2)}) async-start(bf16[8,5,128,896]{3,2,1,0:T(8,128)(2,1)} %bitcast.28), calls=%async_computation | async-start | bytes 18350080 | tf_op jit(solution)/shard_map/all_to_all | solution.py:154
  16.9 2.6 constant_dynamic-slice_fusion.4
  19.5 2.9 %collective-permute-start = (bf16[512,4096]{1,0:T(8,128)(2,1)S(1)}, bf16[512,4096]{1,0:T(8,128)(2,1)}, u32[]{:S(2)}, u32[]{:S(2)}) collective-permute-start(bf16[512,4096]{1,0:T(8,128)(2,1)S(1)} %constant_dynamic-slice_fusion.4), channel_id=1, source_target_pairs={{0,1},{1,0},{2,3},{3,2},{4,5},{5,4},{6,7},{7,6},{8,9},{9,8},{10,11... | collective-permute-start | bytes 12582920 | tf_op jit(solution)/shard_map/ppermute | solution.py:162
  22.5 1.7 fusion
  24.2 11.3 %fusion.5 = bf16[1024,1024]{1,0:T(8,128)(2,1)S(1)} fusion(bf16[4096,1024]{1,0:T(8,128)(2,1)} %param.9, bf16[1024,4096]{1,0:T(8,128)(2,1)S(1)} %copy-done.2, f32[1024]{0:T(1024)S(1)} %add_rsqrt_fusion), kind=kOutput, calls=%fused_computation.10 | convolution fusion | flops 8603566080 | bytes 18878464 | tf_op jit(solution)/shard_map/dot_general | solution.py:168
  38.7 1.6 pad_maximum_fusion
  40.3 73.3 %collective-permute-done.wy_ref = bf16[512,4096]{1,0:T(8,128)(2,1)} collective-permute-done((bf16[512,4096]{1,0:T(8,128)(2,1)S(1)}, bf16[512,4096]{1,0:T(8,128)(2,1)}, u32[]{:S(2)}, u32[]{:S(2)}) %collective-permute-start) | collective-permute-done | bytes 4194336 | tf_op jit(solution)/shard_map/ppermute | solution.py:162
  113.6 6.3 %all-to-all-done = bf16[8,5,128,896]{3,2,1,0:T(8,128)(2,1)} async-done(((bf16[8,5,128,896]{3,2,1,0:T(8,128)(2,1)}), bf16[8,5,128,896]{3,2,1,0:T(8,128)(2,1)}, u32[]{:S(2)}, u32[]{:S(2)}) %all-to-all-start) | async-done | bytes 9175072 | tf_op jit(solution)/shard_map/all_to_all | solution.py:154
  119.9 1.7 collective-permute-start.3
  122.1 10.0 %attend.7 = bf16[4,64,1024]{2,1,0:T(8,128)(2,1)} custom-call(s32[1]{0:T(128)} %bitcast.11.first, s32[32]{0:T(128)} %fusion.11.entries, bf16[16,64,1024]{2,1,0:T(8,128)(2,1)} %bitcast.20, bf16[16,64,1024]{2,1,0:T(8,128)(2,1)} %bitcast.21, bf16[40,128,896]{2,1,0:T(8,128)(2,1)} %bitcast.4.refs_2_.refs_3_.refs_4_.refs_5_, ...), custom_call_target="tpu_custom_call" | custom-call | flops 1000 | bytes 1000 | tf_op jit(solution)/shard_map/attend/pallas_call | solution.py:93
  132.2 2.4 collective-permute-start.4
  134.5 10.0 %attend.5 = bf16[4,64,1024]{2,1,0:T(8,128)(2,1)} custom-call(s32[1]{0:T(128)} %bitcast.7.first, s32[32]{0:T(128)} %fusion.11.entries, bf16[16,64,1024]{2,1,0:T(8,128)(2,1)} %bitcast.22, bf16[16,64,1024]{2,1,0:T(8,128)(2,1)} %bitcast.23, bf16[40,128,896]{2,1,0:T(8,128)(2,1)} %bitcast.4.refs_2_.refs_3_.refs_4_.refs_5_, ...), custom_call_target="tpu_custom_call" | custom-call | flops 1000 | bytes 1000 | tf_op jit(solution)/shard_map/attend/pallas_call | solution.py:93
  144.6 10.0 %attend.6 = bf16[4,64,1024]{2,1,0:T(8,128)(2,1)} custom-call(s32[1]{0:T(128)} %bitcast.9.first, s32[32]{0:T(128)} %fusion.11.entries, bf16[16,64,1024]{2,1,0:T(8,128)(2,1)} %bitcast.24, bf16[16,64,1024]{2,1,0:T(8,128)(2,1)} %bitcast.25, bf16[40,128,896]{2,1,0:T(8,128)(2,1)} %bitcast.4.refs_2_.refs_3_.refs_4_.refs_5_, ...), custom_call_target="tpu_custom_call" | custom-call | flops 1000 | bytes 1000 | tf_op jit(solution)/shard_map/attend/pallas_call | solution.py:93
  154.6 3.7 %collective-permute-done.2 = bf16[4,64,1024]{2,1,0:T(8,128)(2,1)S(1)} collective-permute-done((bf16[4,64,1024]{2,1,0:T(8,128)(2,1)}, bf16[4,64,1024]{2,1,0:T(8,128)(2,1)S(1)}, u32[]{:S(2)}, u32[]{:S(2)}) %collective-permute-start.2) | collective-permute-done | bytes 524320 | tf_op jit(solution)/shard_map/ppermute | solution.py:185
  159.5 10.2 %project.3 = (bf16[192,4096]{1,0:T(8,128)(2,1)S(1)}, bf16[64,4096]{1,0:T(8,128)(2,1)S(1)}) custom-call(bf16[256,1024]{1,0:T(8,128)(2,1)S(1)} %bitcast.18, bf16[256,512]{1,0:T(8,128)(2,1)S(1)} %get-tuple-element.23.y_ref, bf16[256,512]{1,0:T(8,128)(2,1)S(1)} %get-tuple-element.24.z_ref, bf16[1024,4096]{1,0:T(8,128)(2,1)} %wx_ref.3, ...), custom_call_target="tpu_custom_call" | custom-call | flops 1000 | bytes 1000 | tf_op jit(solution)/shard_map/project/pallas_call | solution.py:119
  169.7 2.7 collective-permute-start.7
  172.7 10.0 %attend.4 = bf16[4,64,1024]{2,1,0:T(8,128)(2,1)} custom-call(s32[1]{0:T(128)} %bitcast.first, s32[32]{0:T(128)} %fusion.11.entries, bf16[16,64,1024]{2,1,0:T(8,128)(2,1)} %bitcast.26, bf16[16,64,1024]{2,1,0:T(8,128)(2,1)} %bitcast.27, bf16[40,128,896]{2,1,0:T(8,128)(2,1)} %bitcast.4.refs_2_.refs_3_.refs_4_.refs_5_, ...), custom_call_target="tpu_custom_call" | custom-call | flops 1000 | bytes 1000 | tf_op jit(solution)/shard_map/attend/pallas_call | solution.py:93
  183.8 10.2 %project.2 = (bf16[192,4096]{1,0:T(8,128)(2,1)S(1)}, bf16[64,4096]{1,0:T(8,128)(2,1)S(1)}) custom-call(bf16[256,1024]{1,0:T(8,128)(2,1)S(1)} %bitcast.19, bf16[256,512]{1,0:T(8,128)(2,1)S(1)} %get-tuple-element.20.y_ref, bf16[256,512]{1,0:T(8,128)(2,1)S(1)} %get-tuple-element.19.z_ref, bf16[1024,4096]{1,0:T(8,128)(2,1)} %wx_ref.3, ...), custom_call_target="tpu_custom_call" | custom-call | flops 1000 | bytes 1000 | tf_op jit(solution)/shard_map/project/pallas_call | solution.py:119
  194.0 68.0 %collective-permute-done.5 = bf16[64,4096]{1,0:T(8,128)(2,1)S(1)} collective-permute-done((bf16[64,4096]{1,0:T(8,128)(2,1)S(1)}, bf16[64,4096]{1,0:T(8,128)(2,1)S(1)}, u32[]{:S(2)}, u32[]{:S(2)}) %collective-permute-start.5) | collective-permute-done | bytes 524320 | tf_op jit(solution)/shard_map/ppermute | solution.py:195
  262.3 2.6 collective-permute-start.6
  265.0 1.9 add_convert_fusion
  266.9 9.4 %collective-permute-done.6 = bf16[63,4096]{1,0:T(8,128)(2,1)S(1)} collective-permute-done((bf16[63,4096]{1,0:T(8,128)(2,1)S(1)}, bf16[63,4096]{1,0:T(8,128)(2,1)S(1)}, u32[]{:S(2)}, u32[]{:S(2)}) %collective-permute-start.6) | collective-permute-done | bytes 516128 | tf_op jit(solution)/shard_map/ppermute | solution.py:201
  276.3 1.7 pad_maximum_fusion.1
  (33 shorter events, 9.0 us)
Async XLA Ops:
  11.7 108.2 %all-to-all-start = ((bf16[8,5,128,896]{3,2,1,0:T(8,128)(2,1)}), bf16[8,5,128,896]{3,2,1,0:T(8,128)(2,1)}, u32[]{:S(2)}, u32[]{:S(2)}) async-start(bf16[8,5,128,896]{3,2,1,0:T(8,128)(2,1)} %bitcast.28), calls=%async_computation | async-start | bytes 18350080 | tf_op jit(solution)/shard_map/all_to_all | solution.py:154
  16.9 5.5 %copy-start.2 = (bf16[1024,4096]{1,0:T(8,128)(2,1)S(1)}, bf16[1024,4096]{1,0:T(8,128)(2,1)}, u32[]{:S(2)}) copy-start(bf16[1024,4096]{1,0:T(8,128)(2,1)} %param.8) | copy-start | bytes 25165828
  19.5 94.1 %collective-permute-start = (bf16[512,4096]{1,0:T(8,128)(2,1)S(1)}, bf16[512,4096]{1,0:T(8,128)(2,1)}, u32[]{:S(2)}, u32[]{:S(2)}) collective-permute-start(bf16[512,4096]{1,0:T(8,128)(2,1)S(1)} %constant_dynamic-slice_fusion.4), channel_id=1, source_target_pairs={{0,1},{1,0},{2,3},{3,2},{4,5},{5,4},{6,7},{7,6},{8,9},{9,8},{10,11... | collective-permute-start | bytes 12582920 | tf_op jit(solution)/shard_map/ppermute | solution.py:162
  35.5 3.2 %collective-permute-start.1 = (bf16[63,1024]{1,0:T(8,128)(2,1)S(1)}, bf16[63,1024]{1,0:T(8,128)(2,1)S(1)}, u32[]{:S(2)}, u32[]{:S(2)}) collective-permute-start(bf16[63,1024]{1,0:T(8,128)(2,1)S(1)} %slice.19), channel_id=1, source_target_pairs={{4,0},{8,4},{12,8},{16,12},{20,16},{24,20},{28,24},{5,1},{9,5},{13... | collective-permute-start | bytes 387080 | tf_op jit(solution)/shard_map/ppermute | solution.py:20
  119.9 38.5 %collective-permute-start.3 = (bf16[512,4096]{1,0:T(8,128)(2,1)}, bf16[512,4096]{1,0:T(8,128)(2,1)}, u32[]{:S(2)}, u32[]{:S(2)}) collective-permute-start(bf16[512,4096]{1,0:T(8,128)(2,1)} %collective-permute-done.wy_ref), channel_id=1, source_target_pairs={{0,4},{4,0},{8,12},{12,8},{16,20},{20,16},{24,28},{28,24},{1,5},{5... | collective-permute-start | bytes 12582920 | tf_op jit(solution)/shard_map/ppermute | solution.py:175
  132.2 22.4 %collective-permute-start.4 = (bf16[4,64,1024]{2,1,0:T(8,128)(2,1)}, bf16[4,64,1024]{2,1,0:T(8,128)(2,1)S(1)}, u32[]{:S(2)}, u32[]{:S(2)}) collective-permute-start(bf16[4,64,1024]{2,1,0:T(8,128)(2,1)} %attend.7), channel_id=1, source_target_pairs={{0,1},{1,0},{2,3},{3,2},{4,5},{5,4},{6,7},{7,6},{8,9},{9,8},{10,11... | collective-permute-start | bytes 1572872 | tf_op jit(solution)/shard_map/ppermute | solution.py:185
  144.5 13.8 %collective-permute-start.2 = (bf16[4,64,1024]{2,1,0:T(8,128)(2,1)}, bf16[4,64,1024]{2,1,0:T(8,128)(2,1)S(1)}, u32[]{:S(2)}, u32[]{:S(2)}) collective-permute-start(bf16[4,64,1024]{2,1,0:T(8,128)(2,1)} %attend.5), channel_id=1, source_target_pairs={{0,1},{1,0},{2,3},{3,2},{4,5},{5,4},{6,7},{7,6},{8,9},{9,8},{10,11... | collective-permute-start | bytes 1572872 | tf_op jit(solution)/shard_map/ppermute | solution.py:185
  158.5 1.0 copy-start
  169.7 95.2 %collective-permute-start.7 = (bf16[192,4096]{1,0:T(8,128)(2,1)S(1)}, bf16[192,4096]{1,0:T(8,128)(2,1)}, u32[]{:S(2)}, u32[]{:S(2)}) collective-permute-start(bf16[192,4096]{1,0:T(8,128)(2,1)S(1)} %get-tuple-element.18), channel_id=1, source_target_pairs={{0,2},{1,3},{2,0},{3,1},{4,6},{5,7},{6,4},{7,5},{8,10},{9,11},{10,... | collective-permute-start | bytes 4718600 | tf_op jit(solution)/shard_map/ppermute | solution.py:196
  172.4 89.7 %collective-permute-start.5 = (bf16[64,4096]{1,0:T(8,128)(2,1)S(1)}, bf16[64,4096]{1,0:T(8,128)(2,1)S(1)}, u32[]{:S(2)}, u32[]{:S(2)}) collective-permute-start(bf16[64,4096]{1,0:T(8,128)(2,1)S(1)} %get-tuple-element.16), channel_id=1, source_target_pairs={{0,2},{1,3},{2,0},{3,1},{4,6},{5,7},{6,4},{7,5},{8,10},{9,11},{10,... | collective-permute-start | bytes 1572872 | tf_op jit(solution)/shard_map/ppermute | solution.py:195
  182.7 1.0 copy-start.1
  262.3 13.9 %collective-permute-start.6 = (bf16[63,4096]{1,0:T(8,128)(2,1)S(1)}, bf16[63,4096]{1,0:T(8,128)(2,1)S(1)}, u32[]{:S(2)}, u32[]{:S(2)}) collective-permute-start(bf16[63,4096]{1,0:T(8,128)(2,1)S(1)} %slice.20), channel_id=1, source_target_pairs={{0,1},{1,2},{2,3},{3,4},{4,5},{5,6},{6,7},{7,8},{8,9},{9,10},{10,1... | collective-permute-start | bytes 1548296 | tf_op jit(solution)/shard_map/ppermute | solution.py:201

commit v4 on v3

--- a/solution.py
+++ b/solution.py
@@ -34,20 +34,30 @@
     rows = jnp.concatenate([ref[0] for ref in row_refs], axis=0)
     keys = jnp.dot(rows, wk_ref[...], preferred_element_type=jnp.float32).astype(jnp.bfloat16)
     keys_len, qlen = keys.shape[0] // per_step, q_refs[0].shape[1]
+    pair = 2 * HS if keys.shape[1] % (2 * HS) == 0 else HS
     units = [
-        (place, slice(place * keys_len, (place + 1) * keys_len), slice(at, at + HS))
+        (place, slice(place * keys_len, (place + 1) * keys_len), at)
         for place in range(per_step)
-        for at in range(0, keys.shape[1], HS)
+        for at in range(0, keys.shape[1], pair)
     ]
+    blank = jnp.zeros((qlen, HS), jnp.bfloat16)
+
+    def spread(place, at):
+        if pair == HS:
+            return q_refs[place][0, :, at : at + HS]
+        low = jnp.concatenate([q_refs[place][0, :, at : at + HS], blank], axis=1)
+        high = jnp.concatenate([blank, q_refs[place][0, :, at + HS : at + pair]], axis=1)
+        return jnp.concatenate([low, high], axis=0)
+
     scores = jnp.concatenate(
         [
             lax.dot_general(
-                q_refs[place][0, :, cut],
-                keys[here, cut],
+                spread(place, at),
+                keys[here, at : at + pair],
                 (((1,), (1,)), ((), ())),
                 preferred_element_type=jnp.float32,
             )
-            for place, here, cut in units
+            for place, here, at in units
         ],
         axis=0,
     )
@@ -56,12 +66,17 @@
     weights = jnp.exp((scores - top) * (1.0 / math.sqrt(HS)))
     probs = weights * (1.0 / jnp.sum(weights, axis=-1, keepdims=True))
     probs = probs.astype(jnp.bfloat16)
-    for at, (place, here, cut) in enumerate(units):
-        o_ref[place, :, cut] = jnp.dot(
-            probs[at * qlen : (at + 1) * qlen],
-            values[here, cut],
+    size = qlen * (pair // HS)
+    for unit, (place, here, at) in enumerate(units):
+        mixed = jnp.dot(
+            probs[unit * size : (unit + 1) * size],
+            values[here, at : at + pair],
             preferred_element_type=jnp.float32,
         ).astype(jnp.bfloat16)
+        for part in range(pair // HS):
+            o_ref[place, :, at + part * HS : at + (part + 1) * HS] = mixed[
+                part * qlen : (part + 1) * qlen, part * HS : (part + 1) * HS
+            ]
 
 
 def attend(first, count, entries, queries, rows, w_key, w_value):
@@ -121,12 +136,12 @@
         grid=(features // tile,),
         in_specs=[own(x), own(y), own(z), strip(w_x), strip(w_y), strip(w_z)],
         out_specs=[
-            pl.BlockSpec((size - CL, tile), lambda g: (0, g)),
-            pl.BlockSpec((CL, tile), lambda g: (0, g)),
+            pl.BlockSpec((size // 2, tile), lambda g: (0, g)),
+            pl.BlockSpec((size // 2, tile), lambda g: (0, g)),
         ],
         out_shape=[
-            jax.ShapeDtypeStruct((size - CL, features), jnp.bfloat16),
-            jax.ShapeDtypeStruct((CL, features), jnp.bfloat16),
+            jax.ShapeDtypeStruct((size // 2, features), jnp.bfloat16),
+            jax.ShapeDtypeStruct((size // 2, features), jnp.bfloat16),
         ],
         compiler_params=pltpu.CompilerParams(vmem_limit_bytes=40 * 1024 * 1024),
         cost_estimate=pl.CostEstimate(flops=1000, bytes_accessed=1000, transcendentals=0),
@@ -199,10 +214,10 @@
     last = last.astype(jnp.bfloat16)
     flat = n_seq * n_db
     halo = lax.ppermute(
-        last[1:], ("seq", "db"), [(source, source + 1) for source in range(flat - 1)]
+        last[-(CL - 1) :], ("seq", "db"), [(source, source + 1) for source in range(flat - 1)]
     )
     rest = sum([value.astype(jnp.float32) for value in rests], rest.astype(jnp.float32))
-    return jnp.concatenate([halo, rest.astype(jnp.bfloat16), last[:1]], axis=0)
+    return jnp.concatenate([halo, rest.astype(jnp.bfloat16), last[: -(CL - 1)]], axis=0)
 
 
 def solution(mesh):

time: 282 us -> 277 us (0.982); the launches traced: 278 us -> 277 us
    ppermute x1, waiting for transfers between devices: 0.01 us -> 29.3 us  [body(): rests.append(lax.ppermute(rest, 'db', pairs))]
    ppermute x1, waiting for transfers between devices: 68 us -> 47.4 us  [body(): lasts.append(lax.ppermute(last, 'db', pairs))]
    ppermute x1, waiting for transfers between devices: 9.36 us -> 0.01 us  [body(): lax.ppermute(last[-(CL - 1):], ('seq', 'db'), [(source, source + 1) for s...]
  transfers between devices with their start and end apart: 9 -> 9, of which waited for: 6 -> 6; matrix products, arithmetic and copies ran while one was open for 7% -> 8% of each run, Pallas kernels for 18% -> 18%
where the time goes in v4:
time: 277 us
  waiting for transfers between devices  161 us (58%)
  Pallas kernels  59.8 us (22%)
  starting transfers between devices  18 us (6%)
  local copies, waits for them, and re-layouts  16.7 us (6%)
  matrix products  11.3 us (4%)
  other arithmetic  8.98 us (3%)
    ppermute x1, waiting for transfers between devices, body(): lax.ppermute(lax.dynamic_slice_in_dim(w_out, my_half * half, half, 0), 'd...  73.3 us
    ppermute x1, waiting for transfers between devices, body(): lasts.append(lax.ppermute(last, 'db', pairs))  47.4 us
    pallas_call x4, Pallas kernels, attend(): pl.pallas_call(attend_kernel, grid_spec=grid_spec, out_shape=jax.ShapeDty...  39.3 us
    ppermute x1, waiting for transfers between devices, body(): rests.append(lax.ppermute(rest, 'db', pairs))  29.3 us
    pallas_call x2, Pallas kernels, project(): pl.pallas_call(project_kernel, grid=(features // tile,), in_specs=[own(x)...  20.5 us
    dot_general x1, matrix products, body(): jnp.dot(normed, w_query, preferred_element_type=jnp.float32)  11.3 us
    gather x1, local copies, waits for them, and re-layouts, body(): outgoing = database[send_slot]  9.27 us
    all_to_all x1, waiting for transfers between devices, body(): lax.all_to_all(outgoing, 'seq', split_axis=0, concat_axis=0, tiled=True)  6.29 us
  transfers between devices with their start and end apart: 9, of which 6 were waited for; matrix products, arithmetic and copies ran while one was open for 8% of the time, Pallas kernels for 18%

profile of v4, /device:TPU:0, one launch (start us, length us, event | category | flops | bytes accessed | tf_op | source)
XLA Modules:
  0.0 276.5 jit_solution(11686530487938545277)
XLA Ops:
  2.4 9.3 %gather_fusion = bf16[40,128,896]{2,1,0:T(8,128)(2,1)} fusion(bf16[24,128,896]{2,1,0:T(8,128)(2,1)} %param.13, s32[1024]{0:T(1024)S(1)} %pad_clamp_fusion), kind=kCustom, calls=%fused_computation | custom fusion | bytes 18350240 | tf_op jit(solution)/shard_map/gather | solution.py:168
  11.7 5.2 %all-to-all-start = ((bf16[8,5,128,896]{3,2,1,0:T(8,128)(2,1)}), bf16[8,5,128,896]{3,2,1,0:T(8,128)(2,1)}, u32[]{:S(2)}, u32[]{:S(2)}) async-start(bf16[8,5,128,896]{3,2,1,0:T(8,128)(2,1)} %bitcast.28), calls=%async_computation | async-start | bytes 18350080 | tf_op jit(solution)/shard_map/all_to_all | solution.py:169
  16.9 2.6 constant_dynamic-slice_fusion.4
  19.5 3.0 %collective-permute-start = (bf16[512,4096]{1,0:T(8,128)(2,1)S(1)}, bf16[512,4096]{1,0:T(8,128)(2,1)}, u32[]{:S(2)}, u32[]{:S(2)}) collective-permute-start(bf16[512,4096]{1,0:T(8,128)(2,1)S(1)} %constant_dynamic-slice_fusion.4), channel_id=1, source_target_pairs={{0,1},{1,0},{2,3},{3,2},{4,5},{5,4},{6,7},{7,6},{8,9},{9,8},{10,11... | collective-permute-start | bytes 12582920 | tf_op jit(solution)/shard_map/ppermute | solution.py:177
  22.5 1.7 fusion
  24.2 11.3 %fusion.5 = bf16[1024,1024]{1,0:T(8,128)(2,1)S(1)} fusion(bf16[4096,1024]{1,0:T(8,128)(2,1)} %param.9, bf16[1024,4096]{1,0:T(8,128)(2,1)S(1)} %copy-done.2, f32[1024]{0:T(1024)S(1)} %add_rsqrt_fusion), kind=kOutput, calls=%fused_computation.11 | convolution fusion | flops 8603566080 | bytes 18878464 | tf_op jit(solution)/shard_map/dot_general | solution.py:183
  35.5 1.5 collective-permute-start.1
  38.8 1.6 pad_maximum_fusion
  40.4 73.3 %collective-permute-done.wy_ref = bf16[512,4096]{1,0:T(8,128)(2,1)} collective-permute-done((bf16[512,4096]{1,0:T(8,128)(2,1)S(1)}, bf16[512,4096]{1,0:T(8,128)(2,1)}, u32[]{:S(2)}, u32[]{:S(2)}) %collective-permute-start) | collective-permute-done | bytes 4194336 | tf_op jit(solution)/shard_map/ppermute | solution.py:177
  113.7 6.3 %all-to-all-done = bf16[8,5,128,896]{3,2,1,0:T(8,128)(2,1)} async-done(((bf16[8,5,128,896]{3,2,1,0:T(8,128)(2,1)}), bf16[8,5,128,896]{3,2,1,0:T(8,128)(2,1)}, u32[]{:S(2)}, u32[]{:S(2)}) %all-to-all-start) | async-done | bytes 9175072 | tf_op jit(solution)/shard_map/all_to_all | solution.py:169
  120.0 1.7 collective-permute-start.3
  122.2 9.8 %attend.7 = bf16[4,64,1024]{2,1,0:T(8,128)(2,1)} custom-call(s32[1]{0:T(128)} %bitcast.11.first, s32[32]{0:T(128)} %fusion.11.entries, bf16[16,64,1024]{2,1,0:T(8,128)(2,1)} %bitcast.20, bf16[16,64,1024]{2,1,0:T(8,128)(2,1)} %bitcast.21, bf16[40,128,896]{2,1,0:T(8,128)(2,1)} %bitcast.4.refs_2_.refs_3_.refs_4_.refs_5_, ...), custom_call_target="tpu_custom_call" | custom-call | flops 1000 | bytes 1000 | tf_op jit(solution)/shard_map/attend/pallas_call | solution.py:108
  132.0 2.4 collective-permute-start.4
  134.4 9.8 %attend.5 = bf16[4,64,1024]{2,1,0:T(8,128)(2,1)} custom-call(s32[1]{0:T(128)} %bitcast.7.first, s32[32]{0:T(128)} %fusion.11.entries, bf16[16,64,1024]{2,1,0:T(8,128)(2,1)} %bitcast.22, bf16[16,64,1024]{2,1,0:T(8,128)(2,1)} %bitcast.23, bf16[40,128,896]{2,1,0:T(8,128)(2,1)} %bitcast.4.refs_2_.refs_3_.refs_4_.refs_5_, ...), custom_call_target="tpu_custom_call" | custom-call | flops 1000 | bytes 1000 | tf_op jit(solution)/shard_map/attend/pallas_call | solution.py:108
  144.2 9.9 %attend.6 = bf16[4,64,1024]{2,1,0:T(8,128)(2,1)} custom-call(s32[1]{0:T(128)} %bitcast.9.first, s32[32]{0:T(128)} %fusion.11.entries, bf16[16,64,1024]{2,1,0:T(8,128)(2,1)} %bitcast.24, bf16[16,64,1024]{2,1,0:T(8,128)(2,1)} %bitcast.25, bf16[40,128,896]{2,1,0:T(8,128)(2,1)} %bitcast.4.refs_2_.refs_3_.refs_4_.refs_5_, ...), custom_call_target="tpu_custom_call" | custom-call | flops 1000 | bytes 1000 | tf_op jit(solution)/shard_map/attend/pallas_call | solution.py:108
  154.1 3.9 %collective-permute-done.2 = bf16[4,64,1024]{2,1,0:T(8,128)(2,1)S(1)} collective-permute-done((bf16[4,64,1024]{2,1,0:T(8,128)(2,1)}, bf16[4,64,1024]{2,1,0:T(8,128)(2,1)S(1)}, u32[]{:S(2)}, u32[]{:S(2)}) %collective-permute-start.2) | collective-permute-done | bytes 524320 | tf_op jit(solution)/shard_map/ppermute | solution.py:200
  159.2 10.2 %project.3 = (bf16[128,4096]{1,0:T(8,128)(2,1)S(1)}, bf16[128,4096]{1,0:T(8,128)(2,1)S(1)}) custom-call(bf16[256,1024]{1,0:T(8,128)(2,1)S(1)} %bitcast.18, bf16[256,512]{1,0:T(8,128)(2,1)S(1)} %get-tuple-element.23.y_ref, bf16[256,512]{1,0:T(8,128)(2,1)S(1)} %get-tuple-element.24.z_ref, bf16[1024,4096]{1,0:T(8,128)(2,1)} %wx_ref.3, ...), custom_call_target="tpu_custom_call" | custom-call | flops 1000 | bytes 1000 | tf_op jit(solution)/shard_map/project/pallas_call | solution.py:134
  169.4 2.8 %collective-permute-start.5 = (bf16[128,4096]{1,0:T(8,128)(2,1)S(1)}, bf16[128,4096]{1,0:T(8,128)(2,1)}, u32[]{:S(2)}, u32[]{:S(2)}) collective-permute-start(bf16[128,4096]{1,0:T(8,128)(2,1)S(1)} %get-tuple-element.16), channel_id=1, source_target_pairs={{0,2},{1,3},{2,0},{3,1},{4,6},{5,7},{6,4},{7,5},{8,10},{9,11},{10,... | collective-permute-start | bytes 3145736 | tf_op jit(solution)/shard_map/ppermute | solution.py:210
  172.4 9.8 %attend.4 = bf16[4,64,1024]{2,1,0:T(8,128)(2,1)} custom-call(s32[1]{0:T(128)} %bitcast.first, s32[32]{0:T(128)} %fusion.11.entries, bf16[16,64,1024]{2,1,0:T(8,128)(2,1)} %bitcast.26, bf16[16,64,1024]{2,1,0:T(8,128)(2,1)} %bitcast.27, bf16[40,128,896]{2,1,0:T(8,128)(2,1)} %bitcast.4.refs_2_.refs_3_.refs_4_.refs_5_, ...), custom_call_target="tpu_custom_call" | custom-call | flops 1000 | bytes 1000 | tf_op jit(solution)/shard_map/attend/pallas_call | solution.py:108
  183.3 10.2 %project.2 = (bf16[128,4096]{1,0:T(8,128)(2,1)S(1)}, bf16[128,4096]{1,0:T(8,128)(2,1)S(1)}) custom-call(bf16[256,1024]{1,0:T(8,128)(2,1)S(1)} %bitcast.19, bf16[256,512]{1,0:T(8,128)(2,1)S(1)} %get-tuple-element.20.y_ref, bf16[256,512]{1,0:T(8,128)(2,1)S(1)} %get-tuple-element.19.z_ref, bf16[1024,4096]{1,0:T(8,128)(2,1)} %wx_ref.3, ...), custom_call_target="tpu_custom_call" | custom-call | flops 1000 | bytes 1000 | tf_op jit(solution)/shard_map/project/pallas_call | solution.py:134
  193.6 47.4 %collective-permute-done.5 = bf16[128,4096]{1,0:T(8,128)(2,1)} collective-permute-done((bf16[128,4096]{1,0:T(8,128)(2,1)S(1)}, bf16[128,4096]{1,0:T(8,128)(2,1)}, u32[]{:S(2)}, u32[]{:S(2)}) %collective-permute-start.5) | collective-permute-done | bytes 1048608 | tf_op jit(solution)/shard_map/ppermute | solution.py:210
  241.0 1.5 add_convert_fusion.1
  244.0 29.3 %collective-permute-done.7 = bf16[128,4096]{1,0:T(8,128)(2,1)} collective-permute-done((bf16[128,4096]{1,0:T(8,128)(2,1)S(1)}, bf16[128,4096]{1,0:T(8,128)(2,1)}, u32[]{:S(2)}, u32[]{:S(2)}) %collective-permute-start.7) | collective-permute-done | bytes 1048608 | tf_op jit(solution)/shard_map/ppermute | solution.py:211
  274.8 1.7 pad_maximum_fusion.1
  (33 shorter events, 10.1 us)
Async XLA Ops:
  11.7 108.2 %all-to-all-start = ((bf16[8,5,128,896]{3,2,1,0:T(8,128)(2,1)}), bf16[8,5,128,896]{3,2,1,0:T(8,128)(2,1)}, u32[]{:S(2)}, u32[]{:S(2)}) async-start(bf16[8,5,128,896]{3,2,1,0:T(8,128)(2,1)} %bitcast.28), calls=%async_computation | async-start | bytes 18350080 | tf_op jit(solution)/shard_map/all_to_all | solution.py:169
  16.9 5.6 %copy-start.2 = (bf16[1024,4096]{1,0:T(8,128)(2,1)S(1)}, bf16[1024,4096]{1,0:T(8,128)(2,1)}, u32[]{:S(2)}) copy-start(bf16[1024,4096]{1,0:T(8,128)(2,1)} %param.8) | copy-start | bytes 25165828
  19.5 94.2 %collective-permute-start = (bf16[512,4096]{1,0:T(8,128)(2,1)S(1)}, bf16[512,4096]{1,0:T(8,128)(2,1)}, u32[]{:S(2)}, u32[]{:S(2)}) collective-permute-start(bf16[512,4096]{1,0:T(8,128)(2,1)S(1)} %constant_dynamic-slice_fusion.4), channel_id=1, source_target_pairs={{0,1},{1,0},{2,3},{3,2},{4,5},{5,4},{6,7},{7,6},{8,9},{9,8},{10,11... | collective-permute-start | bytes 12582920 | tf_op jit(solution)/shard_map/ppermute | solution.py:177
  35.5 3.2 %collective-permute-start.1 = (bf16[63,1024]{1,0:T(8,128)(2,1)S(1)}, bf16[63,1024]{1,0:T(8,128)(2,1)S(1)}, u32[]{:S(2)}, u32[]{:S(2)}) collective-permute-start(bf16[63,1024]{1,0:T(8,128)(2,1)S(1)} %slice.19), channel_id=1, source_target_pairs={{4,0},{8,4},{12,8},{16,12},{20,16},{24,20},{28,24},{5,1},{9,5},{13... | collective-permute-start | bytes 387080 | tf_op jit(solution)/shard_map/ppermute | solution.py:20
  120.0 38.2 %collective-permute-start.3 = (bf16[512,4096]{1,0:T(8,128)(2,1)}, bf16[512,4096]{1,0:T(8,128)(2,1)}, u32[]{:S(2)}, u32[]{:S(2)}) collective-permute-start(bf16[512,4096]{1,0:T(8,128)(2,1)} %collective-permute-done.wy_ref), channel_id=1, source_target_pairs={{0,4},{4,0},{8,12},{12,8},{16,20},{20,16},{24,28},{28,24},{1,5},{5... | collective-permute-start | bytes 12582920 | tf_op jit(solution)/shard_map/ppermute | solution.py:190
  132.0 22.1 %collective-permute-start.4 = (bf16[4,64,1024]{2,1,0:T(8,128)(2,1)}, bf16[4,64,1024]{2,1,0:T(8,128)(2,1)S(1)}, u32[]{:S(2)}, u32[]{:S(2)}) collective-permute-start(bf16[4,64,1024]{2,1,0:T(8,128)(2,1)} %attend.7), channel_id=1, source_target_pairs={{0,1},{1,0},{2,3},{3,2},{4,5},{5,4},{6,7},{7,6},{8,9},{9,8},{10,11... | collective-permute-start | bytes 1572872 | tf_op jit(solution)/shard_map/ppermute | solution.py:200
  144.2 13.8 %collective-permute-start.2 = (bf16[4,64,1024]{2,1,0:T(8,128)(2,1)}, bf16[4,64,1024]{2,1,0:T(8,128)(2,1)S(1)}, u32[]{:S(2)}, u32[]{:S(2)}) collective-permute-start(bf16[4,64,1024]{2,1,0:T(8,128)(2,1)} %attend.5), channel_id=1, source_target_pairs={{0,1},{1,0},{2,3},{3,2},{4,5},{5,4},{6,7},{7,6},{8,9},{9,8},{10,11... | collective-permute-start | bytes 1572872 | tf_op jit(solution)/shard_map/ppermute | solution.py:200
  158.1 1.0 copy-start
  169.4 71.6 %collective-permute-start.5 = (bf16[128,4096]{1,0:T(8,128)(2,1)S(1)}, bf16[128,4096]{1,0:T(8,128)(2,1)}, u32[]{:S(2)}, u32[]{:S(2)}) collective-permute-start(bf16[128,4096]{1,0:T(8,128)(2,1)S(1)} %get-tuple-element.16), channel_id=1, source_target_pairs={{0,2},{1,3},{2,0},{3,1},{4,6},{5,7},{6,4},{7,5},{8,10},{9,11},{10,... | collective-permute-start | bytes 3145736 | tf_op jit(solution)/shard_map/ppermute | solution.py:210
  172.2 101.1 %collective-permute-start.7 = (bf16[128,4096]{1,0:T(8,128)(2,1)S(1)}, bf16[128,4096]{1,0:T(8,128)(2,1)}, u32[]{:S(2)}, u32[]{:S(2)}) collective-permute-start(bf16[128,4096]{1,0:T(8,128)(2,1)S(1)} %get-tuple-element.18), channel_id=1, source_target_pairs={{0,2},{1,3},{2,0},{3,1},{4,6},{5,7},{6,4},{7,5},{8,10},{9,11},{10,... | collective-permute-start | bytes 3145736 | tf_op jit(solution)/shard_map/ppermute | solution.py:211
  182.3 1.0 copy-start.1
  242.7 32.1 %collective-permute-start.6 = (bf16[63,4096]{1,0:T(8,128)(2,1)S(1)}, bf16[63,4096]{1,0:T(8,128)(2,1)S(1)}, u32[]{:S(2)}, u32[]{:S(2)}) collective-permute-start(bf16[63,4096]{1,0:T(8,128)(2,1)S(1)} %slice.20), channel_id=1, source_target_pairs={{0,1},{1,2},{2,3},{3,4},{4,5},{5,6},{6,7},{7,8},{8,9},{9,10},{10,1... | collective-permute-start | bytes 1548296 | tf_op jit(solution)/shard_map/ppermute | solution.py:216

commit v5 on v4

--- a/solution.py
+++ b/solution.py
@@ -115,18 +115,18 @@
     )(first.reshape(1).astype(jnp.int32), entries, *operands)
 
 
-def project_kernel(x_ref, y_ref, z_ref, wx_ref, wy_ref, wz_ref, rest_ref, last_ref):
+def project_kernel(x_ref, y_ref, z_ref, wx_ref, wy_ref, wz_ref, *out_refs):
     total = jnp.dot(x_ref[...], wx_ref[...], preferred_element_type=jnp.float32)
     total += jnp.dot(y_ref[...], wy_ref[...], preferred_element_type=jnp.float32)
     total += jnp.dot(z_ref[...], wz_ref[...], preferred_element_type=jnp.float32)
     total = total.astype(jnp.bfloat16)
-    cut = rest_ref.shape[0]
-    rest_ref[...] = total[:cut]
-    last_ref[...] = total[cut:]
-
-
-def project(x, y, z, w_x, w_y, w_z):
-    size, width = x.shape
+    size = out_refs[0].shape[0]
+    for at, ref in enumerate(out_refs):
+        ref[...] = total[at * size : (at + 1) * size]
+
+
+def project(parts, x, y, z, w_x, w_y, w_z):
+    size = x.shape[0] // parts
     features = w_x.shape[1]
     tile = 512
     own = lambda array: pl.BlockSpec(array.shape, lambda g: (0, 0))
@@ -135,14 +135,8 @@
         project_kernel,
         grid=(features // tile,),
         in_specs=[own(x), own(y), own(z), strip(w_x), strip(w_y), strip(w_z)],
-        out_specs=[
-            pl.BlockSpec((size // 2, tile), lambda g: (0, g)),
-            pl.BlockSpec((size // 2, tile), lambda g: (0, g)),
-        ],
-        out_shape=[
-            jax.ShapeDtypeStruct((size // 2, features), jnp.bfloat16),
-            jax.ShapeDtypeStruct((size // 2, features), jnp.bfloat16),
-        ],
+        out_specs=[pl.BlockSpec((size, tile), lambda g: (0, g))] * parts,
+        out_shape=[jax.ShapeDtypeStruct((size, features), jnp.bfloat16)] * parts,
         compiler_params=pltpu.CompilerParams(vmem_limit_bytes=40 * 1024 * 1024),
         cost_estimate=pl.CostEstimate(flops=1000, bytes_accessed=1000, transcendentals=0),
         name="project",
@@ -191,25 +185,35 @@
     blocks = n_db // 2
     block_spans = spans_dev // n_db
 
-    def attend_block(owner, step, queries):
-        first = lax.rem(owner + 2 * step, n_db) * block_spans
-        return attend(first, block_spans, entries, queries, rows, w_key, w_value)
-
-    def partial_of(step, queries):
-        theirs = attend_block(db_index ^ 1, step, queries)
-        from_pair = lax.ppermute(theirs, "db", swap).reshape(-1, width)
-        ours = attend_block(db_index, step, queries)
-        near = lax.dynamic_slice_in_dim(from_pair, my_half * half, half, 1)
-        far = lax.dynamic_slice_in_dim(from_pair, (1 - my_half) * half, half, 1)
-        return project(ours.reshape(-1, width), near, far, w_out, w_near, w_far)
+    half_spans = block_spans // 2
+
+    def context_of(owner, step, inner, count, queries):
+        first = lax.rem(owner + 2 * step, n_db) * block_spans + inner
+        return attend(first, count, entries, queries, rows, w_key, w_value)
+
+    from_pair = {}
+    for step in [*range(1, blocks), 0]:
+        theirs = context_of(db_index ^ 1, step, 0, block_spans, aligned_queries)
+        theirs, aligned_queries = lax.optimization_barrier((theirs, aligned_queries))
+        from_pair[step] = lax.ppermute(theirs, "db", swap)
+
+    def partial_of(step, inner, count, queries):
+        ours = context_of(db_index, step, inner, count, queries).reshape(-1, width)
+        other = from_pair[step][inner : inner + count].reshape(-1, width)
+        near = lax.dynamic_slice_in_dim(other, my_half * half, half, 1)
+        far = lax.dynamic_slice_in_dim(other, (1 - my_half) * half, half, 1)
+        return project(count // half_spans, ours, near, far, w_out, w_near, w_far)
 
     rests, lasts = [], []
     for step in range(1, blocks):
-        rest, last = partial_of(step, aligned_queries)
         pairs = [(source, (source + 2 * step) % n_db) for source in range(n_db)]
-        lasts.append(lax.ppermute(last, "db", pairs))
-        rests.append(lax.ppermute(rest, "db", pairs))
-    rest, last = partial_of(0, aligned_queries)
+        for inner, sums in ((half_spans, lasts), (0, rests)):
+            (partial,) = partial_of(step, inner, half_spans, aligned_queries)
+            partial, aligned_queries, from_pair[0] = lax.optimization_barrier(
+                (partial, aligned_queries, from_pair[0])
+            )
+            sums.append(lax.ppermute(partial, "db", pairs))
+    rest, last = partial_of(0, 0, block_spans, aligned_queries)
     last = sum([value.astype(jnp.float32) for value in lasts], last.astype(jnp.float32))
     last = last.astype(jnp.bfloat16)
     flat = n_seq * n_db

time: 277 us -> 269 us (0.971)
  waiting for transfers between devices: 161 us -> 142 us
  Pallas kernels: 59.8 us -> 71.6 us
    ppermute x4, waiting for transfers between devices: 80.6 us -> 61.4 us  [the longest x2 61.4 us: body(): sums.append(lax.ppermute(partial, 'db', pairs))]
    pallas_call x2 -> x3, Pallas kernels: 20.5 us -> 28.4 us  [project(): pl.pallas_call(project_kernel, grid=(features // tile,), in_specs=[own(x)...]
    pallas_call x4 -> x5, Pallas kernels: 39.3 us -> 43.2 us  [attend(): pl.pallas_call(attend_kernel, grid_spec=grid_spec, out_shape=jax.ShapeDty...]
  transfers between devices with their start and end apart: 9 -> 9, of which waited for: 6 -> 5; matrix products, arithmetic and copies ran while one was open for 8% -> 7% of each run, Pallas kernels for 18% -> 27%
where the time goes in v5:
time: 269 us; the launch traced here: 268 us
  waiting for transfers between devices  142 us (53%)
  Pallas kernels  71.6 us (27%)
  starting transfers between devices  18.3 us (7%)
  local copies, waits for them, and re-layouts  17.5 us (7%)
  matrix products  11.3 us (4%)
  other arithmetic  6.6 us (2%)
    ppermute x1, waiting for transfers between devices, body(): lax.ppermute(lax.dynamic_slice_in_dim(w_out, my_half * half, half, 0), 'd...  73.3 us
    ppermute x2, waiting for transfers between devices, body(): sums.append(lax.ppermute(partial, 'db', pairs))  61.4 us
    pallas_call x5, Pallas kernels, attend(): pl.pallas_call(attend_kernel, grid_spec=grid_spec, out_shape=jax.ShapeDty...  43.2 us
    pallas_call x3, Pallas kernels, project(): pl.pallas_call(project_kernel, grid=(features // tile,), in_specs=[own(x)...  28.4 us
    dot_general x1, matrix products, body(): jnp.dot(normed, w_query, preferred_element_type=jnp.float32)  11.3 us
    gather x1, local copies, waits for them, and re-layouts, body(): outgoing = database[send_slot]  9.28 us
    all_to_all x1, waiting for transfers between devices, body(): lax.all_to_all(outgoing, 'seq', split_axis=0, concat_axis=0, tiled=True)  6.22 us
  transfers between devices with their start and end apart: 9, of which 5 were waited for; matrix products, arithmetic and copies ran while one was open for 7% of the time, Pallas kernels for 27%

profile of v5, /device:TPU:0, one launch (start us, length us, event | category | flops | bytes accessed | tf_op | source)
XLA Modules:
  0.0 267.9 jit_solution(12267658745155080134)
XLA Ops:
  2.4 9.3 %gather_fusion = bf16[40,128,896]{2,1,0:T(8,128)(2,1)} fusion(bf16[24,128,896]{2,1,0:T(8,128)(2,1)} %param.13, s32[1024]{0:T(1024)S(1)} %pad_clamp_fusion), kind=kCustom, calls=%fused_computation | custom fusion | bytes 18350240 | tf_op jit(solution)/shard_map/gather | solution.py:162
  11.7 5.2 %all-to-all-start = ((bf16[8,5,128,896]{3,2,1,0:T(8,128)(2,1)}), bf16[8,5,128,896]{3,2,1,0:T(8,128)(2,1)}, u32[]{:S(2)}, u32[]{:S(2)}) async-start(bf16[8,5,128,896]{3,2,1,0:T(8,128)(2,1)} %bitcast.34), calls=%async_computation | async-start | bytes 18350080 | tf_op jit(solution)/shard_map/all_to_all | solution.py:163
  16.9 2.6 constant_dynamic-slice_fusion.6
  19.5 3.0 %collective-permute-start = (bf16[512,4096]{1,0:T(8,128)(2,1)S(1)}, bf16[512,4096]{1,0:T(8,128)(2,1)}, u32[]{:S(2)}, u32[]{:S(2)}) collective-permute-start(bf16[512,4096]{1,0:T(8,128)(2,1)S(1)} %constant_dynamic-slice_fusion.6), channel_id=1, source_target_pairs={{0,1},{1,0},{2,3},{3,2},{4,5},{5,4},{6,7},{7,6},{8,9},{9,8},{10,11... | collective-permute-start | bytes 12582920 | tf_op jit(solution)/shard_map/ppermute | solution.py:171
  22.5 1.7 fusion
  24.2 11.3 %fusion.5 = bf16[1024,1024]{1,0:T(8,128)(2,1)S(1)} fusion(bf16[4096,1024]{1,0:T(8,128)(2,1)} %param.9, bf16[1024,4096]{1,0:T(8,128)(2,1)S(1)} %copy-done.3, f32[1024]{0:T(1024)S(1)} %add_rsqrt_fusion), kind=kOutput, calls=%fused_computation.11 | convolution fusion | flops 8603566080 | bytes 18878464 | tf_op jit(solution)/shard_map/dot_general | solution.py:177
  38.8 1.6 pad_maximum_fusion
  40.4 73.3 %collective-permute-done.wy_ref = bf16[512,4096]{1,0:T(8,128)(2,1)} collective-permute-done((bf16[512,4096]{1,0:T(8,128)(2,1)S(1)}, bf16[512,4096]{1,0:T(8,128)(2,1)}, u32[]{:S(2)}, u32[]{:S(2)}) %collective-permute-start) | collective-permute-done | bytes 4194336 | tf_op jit(solution)/shard_map/ppermute | solution.py:171
  113.7 6.2 %all-to-all-done = bf16[8,5,128,896]{3,2,1,0:T(8,128)(2,1)} async-done(((bf16[8,5,128,896]{3,2,1,0:T(8,128)(2,1)}), bf16[8,5,128,896]{3,2,1,0:T(8,128)(2,1)}, u32[]{:S(2)}, u32[]{:S(2)}) %all-to-all-start) | async-done | bytes 9175072 | tf_op jit(solution)/shard_map/all_to_all | solution.py:163
  119.9 1.7 collective-permute-start.3
  122.2 10.0 %attend.5 = bf16[4,64,1024]{2,1,0:T(8,128)(2,1)} custom-call(s32[1]{0:T(128)} %bitcast.5.first, s32[32]{0:T(128)} %fusion.11.entries, bf16[16,64,1024]{2,1,0:T(8,128)(2,1)} %bitcast.24, bf16[16,64,1024]{2,1,0:T(8,128)(2,1)} %bitcast.25, bf16[40,128,896]{2,1,0:T(8,128)(2,1)} %bitcast.8.refs_2_.refs_3_.refs_4_.refs_5_, ...), custom_call_target="tpu_custom_call" | custom-call | flops 1000 | bytes 1000 | tf_op jit(solution)/shard_map/attend/pallas_call | solution.py:108
  132.2 2.5 collective-permute-start.2
  134.7 9.8 %attend.6 = bf16[4,64,1024]{2,1,0:T(8,128)(2,1)} custom-call(s32[1]{0:T(128)} %bitcast.4.first, s32[32]{0:T(128)} %fusion.11.entries, bf16[16,64,1024]{2,1,0:T(8,128)(2,1)} %bitcast.26, bf16[16,64,1024]{2,1,0:T(8,128)(2,1)} %bitcast.27, bf16[40,128,896]{2,1,0:T(8,128)(2,1)} %bitcast.8.refs_2_.refs_3_.refs_4_.refs_5_, ...), custom_call_target="tpu_custom_call" | custom-call | flops 1000 | bytes 1000 | tf_op jit(solution)/shard_map/attend/pallas_call | solution.py:108
  144.5 6.7 %attend.7 = bf16[2,64,1024]{2,1,0:T(8,128)(2,1)} custom-call(s32[1]{0:T(128)} %bitcast.3.first, s32[32]{0:T(128)} %fusion.11.entries, bf16[16,64,1024]{2,1,0:T(8,128)(2,1)} %bitcast.28, bf16[16,64,1024]{2,1,0:T(8,128)(2,1)} %bitcast.29, bf16[40,128,896]{2,1,0:T(8,128)(2,1)} %bitcast.8.refs_2_.refs_3_.refs_4_.refs_5_, ...), custom_call_target="tpu_custom_call" | custom-call | flops 1000 | bytes 1000 | tf_op jit(solution)/shard_map/attend/pallas_call | solution.py:108
  152.3 9.1 %project.3 = bf16[128,4096]{1,0:T(8,128)(2,1)S(1)} custom-call(bf16[128,1024]{1,0:T(8,128)(2,1)S(1)} %bitcast.22, bf16[128,512]{1,0:T(8,128)(2,1)S(1)} %get-tuple-element.43.y_ref, bf16[128,512]{1,0:T(8,128)(2,1)S(1)} %get-tuple-element.44.z_ref, bf16[1024,4096]{1,0:T(8,128)(2,1)} %wx_ref.5, bf16[512,4096]{1,0:T(8,128)(2,1)} %collective-permute-done.wy_ref, ...), custom_call_target="tpu_custom_call" | custom-call | flops 1000 | bytes 1000 | tf_op jit(solution)/shard_map/project/pallas_call | solution.py:134
  161.4 3.1 %collective-permute-start.5 = (bf16[128,4096]{1,0:T(8,128)(2,1)S(1)}, bf16[128,4096]{1,0:T(8,128)(2,1)S(1)}, u32[]{:S(2)}, u32[]{:S(2)}) collective-permute-start(bf16[128,4096]{1,0:T(8,128)(2,1)S(1)} %project.3), channel_id=1, source_target_pairs={{0,2},{1,3},{2,0},{3,1},{4,6},{5,7},{6,4},{7,5},{8,10},{9,11},{10,... | collective-permute-start | bytes 3145736 | tf_op jit(solution)/shard_map/ppermute | solution.py:215
  164.5 6.7 %attend.8 = bf16[2,64,1024]{2,1,0:T(8,128)(2,1)} custom-call(s32[1]{0:T(128)} %bitcast.2.first, s32[32]{0:T(128)} %fusion.11.entries, bf16[16,64,1024]{2,1,0:T(8,128)(2,1)} %bitcast.30, bf16[16,64,1024]{2,1,0:T(8,128)(2,1)} %bitcast.31, bf16[40,128,896]{2,1,0:T(8,128)(2,1)} %bitcast.8.refs_2_.refs_3_.refs_4_.refs_5_, ...), custom_call_target="tpu_custom_call" | custom-call | flops 1000 | bytes 1000 | tf_op jit(solution)/shard_map/attend/pallas_call | solution.py:108
  172.2 9.1 %project.4 = bf16[128,4096]{1,0:T(8,128)(2,1)S(1)} custom-call(bf16[128,1024]{1,0:T(8,128)(2,1)S(1)} %bitcast.23, bf16[128,512]{1,0:T(8,128)(2,1)S(1)} %get-tuple-element.40.y_ref, bf16[128,512]{1,0:T(8,128)(2,1)S(1)} %get-tuple-element.39.z_ref, bf16[1024,4096]{1,0:T(8,128)(2,1)} %wx_ref.5, bf16[512,4096]{1,0:T(8,128)(2,1)} %collective-permute-done.wy_ref, ...), custom_call_target="tpu_custom_call" | custom-call | flops 1000 | bytes 1000 | tf_op jit(solution)/shard_map/project/pallas_call | solution.py:134
  181.4 9.8 %attend.9 = bf16[4,64,1024]{2,1,0:T(8,128)(2,1)} custom-call(s32[1]{0:T(128)} %bitcast.first, s32[32]{0:T(128)} %fusion.11.entries, bf16[16,64,1024]{2,1,0:T(8,128)(2,1)} %bitcast.32, bf16[16,64,1024]{2,1,0:T(8,128)(2,1)} %bitcast.33, bf16[40,128,896]{2,1,0:T(8,128)(2,1)} %bitcast.8.refs_2_.refs_3_.refs_4_.refs_5_, ...), custom_call_target="tpu_custom_call" | custom-call | flops 1000 | bytes 1000 | tf_op jit(solution)/shard_map/attend/pallas_call | solution.py:108
  192.3 10.2 %project.5 = (bf16[128,4096]{1,0:T(8,128)(2,1)S(1)}, bf16[128,4096]{1,0:T(8,128)(2,1)S(1)}) custom-call(bf16[256,1024]{1,0:T(8,128)(2,1)S(1)} %bitcast.21, bf16[256,512]{1,0:T(8,128)(2,1)S(1)} %get-tuple-element.36.y_ref, bf16[256,512]{1,0:T(8,128)(2,1)S(1)} %get-tuple-element.35.z_ref, bf16[1024,4096]{1,0:T(8,128)(2,1)} %wx_ref.5, ...), custom_call_target="tpu_custom_call" | custom-call | flops 1000 | bytes 1000 | tf_op jit(solution)/shard_map/project/pallas_call | solution.py:134
  202.6 30.8 %collective-permute-done.5 = bf16[128,4096]{1,0:T(8,128)(2,1)S(1)} collective-permute-done((bf16[128,4096]{1,0:T(8,128)(2,1)S(1)}, bf16[128,4096]{1,0:T(8,128)(2,1)S(1)}, u32[]{:S(2)}, u32[]{:S(2)}) %collective-permute-start.5) | collective-permute-done | bytes 1048608 | tf_op jit(solution)/shard_map/ppermute | solution.py:215
  233.9 1.6 collective-permute-start.6
  235.4 30.5 %collective-permute-done.7 = bf16[128,4096]{1,0:T(8,128)(2,1)S(1)} collective-permute-done((bf16[128,4096]{1,0:T(8,128)(2,1)S(1)}, bf16[128,4096]{1,0:T(8,128)(2,1)S(1)}, u32[]{:S(2)}, u32[]{:S(2)}) %collective-permute-start.7) | collective-permute-done | bytes 1048608 | tf_op jit(solution)/shard_map/ppermute | solution.py:215
  266.2 1.7 pad_maximum_fusion.1
  (39 shorter events, 10.1 us)
Async XLA Ops:
  11.7 108.2 %all-to-all-start = ((bf16[8,5,128,896]{3,2,1,0:T(8,128)(2,1)}), bf16[8,5,128,896]{3,2,1,0:T(8,128)(2,1)}, u32[]{:S(2)}, u32[]{:S(2)}) async-start(bf16[8,5,128,896]{3,2,1,0:T(8,128)(2,1)} %bitcast.34), calls=%async_computation | async-start | bytes 18350080 | tf_op jit(solution)/shard_map/all_to_all | solution.py:163
  16.9 5.6 %copy-start.3 = (bf16[1024,4096]{1,0:T(8,128)(2,1)S(1)}, bf16[1024,4096]{1,0:T(8,128)(2,1)}, u32[]{:S(2)}) copy-start(bf16[1024,4096]{1,0:T(8,128)(2,1)} %param.8) | copy-start | bytes 25165828
  19.5 94.2 %collective-permute-start = (bf16[512,4096]{1,0:T(8,128)(2,1)S(1)}, bf16[512,4096]{1,0:T(8,128)(2,1)}, u32[]{:S(2)}, u32[]{:S(2)}) collective-permute-start(bf16[512,4096]{1,0:T(8,128)(2,1)S(1)} %constant_dynamic-slice_fusion.6), channel_id=1, source_target_pairs={{0,1},{1,0},{2,3},{3,2},{4,5},{5,4},{6,7},{7,6},{8,9},{9,8},{10,11... | collective-permute-start | bytes 12582920 | tf_op jit(solution)/shard_map/ppermute | solution.py:171
  35.5 3.2 %collective-permute-start.1 = (bf16[63,1024]{1,0:T(8,128)(2,1)S(1)}, bf16[63,1024]{1,0:T(8,128)(2,1)S(1)}, u32[]{:S(2)}, u32[]{:S(2)}) collective-permute-start(bf16[63,1024]{1,0:T(8,128)(2,1)S(1)} %slice.27), channel_id=1, source_target_pairs={{4,0},{8,4},{12,8},{16,12},{20,16},{24,20},{28,24},{5,1},{9,5},{13... | collective-permute-start | bytes 387080 | tf_op jit(solution)/shard_map/ppermute | solution.py:20
  119.9 31.5 %collective-permute-start.3 = (bf16[512,4096]{1,0:T(8,128)(2,1)}, bf16[512,4096]{1,0:T(8,128)(2,1)}, u32[]{:S(2)}, u32[]{:S(2)}) collective-permute-start(bf16[512,4096]{1,0:T(8,128)(2,1)} %collective-permute-done.wy_ref), channel_id=1, source_target_pairs={{0,4},{4,0},{8,12},{12,8},{16,20},{20,16},{24,28},{28,24},{1,5},{5... | collective-permute-start | bytes 12582920 | tf_op jit(solution)/shard_map/ppermute | solution.py:184
  132.2 19.0 %collective-permute-start.2 = (bf16[4,64,1024]{2,1,0:T(8,128)(2,1)}, bf16[4,64,1024]{2,1,0:T(8,128)(2,1)S(1)}, u32[]{:S(2)}, u32[]{:S(2)}) collective-permute-start(bf16[4,64,1024]{2,1,0:T(8,128)(2,1)} %attend.5), channel_id=1, source_target_pairs={{0,1},{1,0},{2,3},{3,2},{4,5},{5,4},{6,7},{7,6},{8,9},{9,8},{10,11... | collective-permute-start | bytes 1572872 | tf_op jit(solution)/shard_map/ppermute | solution.py:198
  144.5 16.9 %collective-permute-start.4 = (bf16[4,64,1024]{2,1,0:T(8,128)(2,1)}, bf16[4,64,1024]{2,1,0:T(8,128)(2,1)S(1)}, u32[]{:S(2)}, u32[]{:S(2)}) collective-permute-start(bf16[4,64,1024]{2,1,0:T(8,128)(2,1)} %attend.6), channel_id=1, source_target_pairs={{0,1},{1,0},{2,3},{3,2},{4,5},{5,4},{6,7},{7,6},{8,9},{9,8},{10,11... | collective-permute-start | bytes 1572872 | tf_op jit(solution)/shard_map/ppermute | solution.py:198
  151.4 1.0 copy-start.1
  161.4 72.0 %collective-permute-start.5 = (bf16[128,4096]{1,0:T(8,128)(2,1)S(1)}, bf16[128,4096]{1,0:T(8,128)(2,1)S(1)}, u32[]{:S(2)}, u32[]{:S(2)}) collective-permute-start(bf16[128,4096]{1,0:T(8,128)(2,1)S(1)} %project.3), channel_id=1, source_target_pairs={{0,2},{1,3},{2,0},{3,1},{4,6},{5,7},{6,4},{7,5},{8,10},{9,11},{10,... | collective-permute-start | bytes 3145736 | tf_op jit(solution)/shard_map/ppermute | solution.py:215
  171.3 0.9 copy-start.2
  181.3 84.6 %collective-permute-start.7 = (bf16[128,4096]{1,0:T(8,128)(2,1)S(1)}, bf16[128,4096]{1,0:T(8,128)(2,1)S(1)}, u32[]{:S(2)}, u32[]{:S(2)}) collective-permute-start(bf16[128,4096]{1,0:T(8,128)(2,1)S(1)} %project.4), channel_id=1, source_target_pairs={{0,2},{1,3},{2,0},{3,1},{4,6},{5,7},{6,4},{7,5},{8,10},{9,11},{10,... | collective-permute-start | bytes 3145736 | tf_op jit(solution)/shard_map/ppermute | solution.py:215
  191.3 1.0 copy-start
  233.9 32.3 %collective-permute-start.6 = (bf16[63,4096]{1,0:T(8,128)(2,1)S(1)}, bf16[63,4096]{1,0:T(8,128)(2,1)S(1)}, u32[]{:S(2)}, u32[]{:S(2)}) collective-permute-start(bf16[63,4096]{1,0:T(8,128)(2,1)S(1)} %slice.30), channel_id=1, source_target_pairs={{0,1},{1,2},{2,3},{3,4},{4,5},{5,6},{6,7},{7,8},{8,9},{9,10},{10,1... | collective-permute-start | bytes 1548296 | tf_op jit(solution)/shard_map/ppermute | solution.py:220
